TPU v7x, 32 devices: a whole 2x2x4 slice. The times are simulated.
32 devices in a mesh: groups: 2 (over y), blk: 4 (over z), pair: 2 (over x), sub: 2 (over core).
Axes of the slice: x: 2, y: 2, z: 4, core: 2. Of those that a mesh axis runs over, the one named last changes fastest.
Arguments:
- generated: bfloat16 [4096, 512], P(('groups', 'blk', 'pair', 'sub')), parts along dimension 0, may hold values from -16 to 16, as said below
- real: bfloat16 [512, 512], P(('groups', 'blk', 'pair', 'sub')), parts along dimension 0, may hold values from -16 to 16, as said below
Outputs:
- gradient: float32 [4096, 512], P(('groups', 'blk', 'pair', 'sub')), parts along dimension 0
- loss: float32 [2], P('groups'), parts along dimension 0
There are 2 independent parts, one for each index of `groups`. A program takes and returns all parts, laid end to end along the dimension named above; each array names one. Nothing has to cross between parts.
Inputs may be any that keep to these rules, and one draw needn't show every extreme that they name: `generated`: generated latents, no further structure promised. `real`: real latents, no further structure promised.
All inputs are finite; a program needn't handle non-finite values.
Results may differ from a plain program's by a relative error of at most 0.0023.
Values may be sent and summed in bfloat16 or wider, within the bound.
No kernel may reach another device: no remote copies, remote signals or barrier semaphores. Data moves between devices by JAX's collectives and lax.ppermute only.
A program may use at most 64 MiB of HBM per device.

v0:
```python
import jax
import jax.numpy as jnp
from jax import lax
from jax.sharding import PartitionSpec as P


def passed_along(shard, axis, by):
    size = lax.axis_size(axis)
    return lax.ppermute(shard, axis, [(i, (i + by) % size) for i in range(size)])


def pair_dist(home, home_sq, other):
    other_sq = jnp.sum(jnp.square(other.astype(jnp.float32)), axis=1)
    gram = lax.dot_general(
        home, other, (((1,), (1,)), ((), ())), preferred_element_type=jnp.float32
    )
    spread = jnp.maximum(home_sq[:, None] + other_sq[None, :] - 2.0 * gram, 0.0)
    return jnp.sqrt(spread / home.shape[1] + 1.0)


def home_term(home, dist, other, factor):
    weight = 1.0 / dist
    pulled = jnp.dot(weight.astype(jnp.bfloat16), other, preferred_element_type=jnp.float32)
    return (factor * (home.astype(jnp.float32) * jnp.sum(weight, axis=1)[:, None] - pulled), weight)


def other_term(home, weight, other, factor):
    pulled = lax.dot_general(
        weight.astype(jnp.bfloat16),
        home,
        (((0,), (0,)), ((), ())),
        preferred_element_type=jnp.float32,
    )
    return factor * (other.astype(jnp.float32) * jnp.sum(weight, axis=0)[:, None] - pulled)


def shards(generated, real):
    cycle_size = lax.axis_size("blk")
    half_way = cycle_size // 2
    devices_all = lax.axis_size(("blk", "pair", "sub"))
    inv_g = 1.0 / (generated.shape[0] * devices_all)
    inv_r = 1.0 / (real.shape[0] * devices_all)
    home = lax.all_gather(generated, ("pair", "sub"), axis=0, tiled=True)
    home_sq = jnp.sum(jnp.square(home.astype(jnp.float32)), axis=1)
    dist = pair_dist(home, home_sq, generated)
    sums, weight = home_term(home, dist, generated, -inv_g)
    loss_part = -jnp.sum(dist) * inv_g * inv_g

    def sym_step(index, carry):
        visitor, partner, acc_sums, acc_loss = carry
        visitor = passed_along(visitor, "blk", 1)
        step_dist = pair_dist(home, home_sq, visitor)
        term, step_weight = home_term(home, step_dist, visitor, -inv_g)
        partner = partner + other_term(home, step_weight, visitor, -inv_g)
        partner = passed_along(partner, "blk", 1)
        return (
            visitor,
            partner,
            acc_sums + term,
            acc_loss - 2.0 * jnp.sum(step_dist) * inv_g * inv_g,
        )

    start_partner = jnp.zeros(generated.shape, jnp.float32)
    visitor, partner, sums, loss_part = lax.fori_loop(
        0, half_way - 1, sym_step, (generated, start_partner, sums, loss_part)
    )
    visitor = passed_along(visitor, "blk", 1)
    last_dist = pair_dist(home, home_sq, visitor)
    term, last_weight = home_term(home, last_dist, visitor, -inv_g)
    sums = sums + term
    loss_part = loss_part - jnp.sum(last_dist) * inv_g * inv_g
    partner = passed_along(partner, "blk", cycle_size - half_way)
    carry = (sums, loss_part)
    piece = lax.all_gather(real, "blk", axis=0, tiled=True)
    real_dist = pair_dist(home, home_sq, piece)
    term, real_weight = home_term(home, real_dist, piece, inv_r)
    sums = carry[0] + term
    loss_part = carry[1] + 2.0 * jnp.sum(real_dist) * inv_g * inv_r
    own_rows = lax.psum_scatter(sums, ("pair", "sub"), scatter_dimension=0, tiled=True)
    total_loss = lax.psum(loss_part, ("blk", "pair", "sub"))
    return (own_rows + partner, total_loss.reshape(1))


def solution(mesh):
    in_specs = (
        P(("groups", "blk", "pair", "sub"), None),
        P(("groups", "blk", "pair", "sub"), None),
    )
    out_specs = (P(("groups", "blk", "pair", "sub"), None), P("groups"))
    return jax.shard_map(shards, mesh=mesh, in_specs=in_specs, out_specs=out_specs, check_vma=False)
```

profile of v0, /device:TPU:0, one launch (start us, length us, event | category | flops | bytes accessed | tf_op | source)
XLA Modules:
  0.0 97.1 jit_solution(15406492886159091549)
XLA Ops:
  7.2 0.0 copy-start
  7.2 0.0 reduce-scatter.2.cloned.1.call-start
  7.2 3.1 %collective-permute-start = (bf16[128,512]{1,0:T(8,128)(2,1)}, bf16[128,512]{1,0:T(8,128)(2,1)S(1)}, u32[]{:S(2)}, u32[]{:S(2)}) collective-permute-start(bf16[128,512]{1,0:T(8,128)(2,1)} %param.2), channel_id=1, source_target_pairs={{0,4},{4,8},{8,12},{12,0},{1,5},{5,9},{9,13},{13,1},{2,6},{6,10},{... | collective-permute-start | bytes 393224 | tf_op jit(solution)/shard_map/while/body/eval_jaxpr/ppermute | solution.py:9
  10.3 7.4 %all_gather.6 = bf16[512,512]{1,0:T(8,128)(2,1)S(1)} all-gather(bf16[128,512]{1,0:T(8,128)(2,1)} %param.2), channel_id=1, replica_groups=mesh['groups'=2,'blk'=4,'pair'=2,'sub'=2] {'pair','sub'}, dimensions={0}, use_global_device_ids=true | all-gather | bytes 655360 | tf_op jit(solution)/shard_map/all_gather | solution.py:43
  17.7 0.0 copy-done
  17.7 0.0 copy-start.1
  17.7 0.1 multiply_reduce_fusion.1
  17.8 0.6 copy-done.1
  18.4 13.3 %all_gather.7 = bf16[64,512]{1,0:T(8,128)(2,1)S(1)} all-gather(bf16[16,512]{1,0:T(8,128)(2,1)S(1)} %copy-done.1), channel_id=1, replica_groups=mesh['groups'=2,'blk'=4,'pair'=2,'sub'=2] {'blk'}, dimensions={0}, use_global_device_ids=true | all-gather | bytes 81920 | tf_op jit(solution)/shard_map/all_gather | solution.py:74
  31.7 0.1 multiply_reduce_fusion.2
  31.8 0.2 fusion.15
  32.0 1.1 %fusion.37 = (f32[]{:T(128)}, f32[512]{0:T(512)S(1)}, f32[512,128]{0,1:T(8,128)S(1)}) fusion(bf16[512,512]{1,0:T(8,128)(2,1)S(1)} %all_gather.6, bf16[128,512]{1,0:T(8,128)(2,1)S(1)} %copy-done, f32[128]{0:T(128)S(1)} %multiply_reduce_fusion.1, f32[512]{0:T(512)S(1)} %fusion.15), kind=kOutput, calls=%fused_computation.56 | convolution fusion | flops 67698176 | bytes 922116 | tf_op jit(solution)/shard_map/dot_general | solution.py:14
  33.1 0.3 convolution_subtract_fusion.3
  33.4 1.0 fusion.39
  34.4 0.0 collective-permute-done
  34.4 0.2 collective-permute-start.1
  34.6 0.3 fusion
  34.9 0.1 fusion.16
  35.1 6.1 %collective-permute-done.1 = bf16[128,512]{1,0:T(8,128)(2,1)S(1)} collective-permute-done((bf16[128,512]{1,0:T(8,128)(2,1)S(1)}, bf16[128,512]{1,0:T(8,128)(2,1)S(1)}, u32[]{:S(2)}, u32[]{:S(2)}) %collective-permute-start.1) | collective-permute-done | bytes 131104 | tf_op jit(solution)/shard_map/ppermute | solution.py:9
  41.1 0.3 convolution_multiply_fusion
  41.5 0.1 multiply_reduce_fusion
  41.6 1.1 %fusion.21 = (f32[]{:T(128)}, f32[512]{0:T(512)S(1)}, f32[]{:T(128)}, f32[512]{0:T(512)S(1)}, f32[128]{0:T(128)S(1)}, /*index=5*/bf16[512,128]{0,1:T(8,128)(2,1)S(1)}) fusion(f32[512,128]{0,1:T(8,128)S(1)} %convolution_multiply_fusion, f32[128]{0:T(128)S(1)} %multiply_reduce_fusion, f32[512]{0:T(512)S(1)} %fusion.15, f32[128]{0:T(128)S(1)} %fusion.16, ...), kind=kOutput, calls=%fused_computation.40 | convolution fusion | flops 68352896 | bytes 1056264 | tf_op jit(solution)/shard_map/while/body/eval_jaxpr/dot_general | solution.py:14
  42.7 0.3 fusion.1
  43.0 1.5 %fusion.4 = f32[512,512]{1,0:T(8,128)} fusion(f32[512,512]{1,0:T(8,128)S(1)} %fusion, f32[512,512]{1,0:T(8,128)S(1)} %fusion.1, bf16[128,512]{1,0:T(8,128)(2,1)S(1)} %collective-permute-done.1, bf16[512,512]{1,0:T(8,128)(2,1)S(1)} %all_gather.6, f32[512]{0:T(512)S(1)} %get-tuple-element.17, f32[512,128]{0,1:T(8,128)S(1)} %convolution_multiply_fusion, ...), kind=kOutput, calls=%fused_computation.13 | convolution fusion | flops 69140480 | bytes 4067840 | tf_op jit(solution)/shard_map/dot_general | solution.py:23
  44.5 0.0 reduce-scatter.2.cloned.1.call-update
  44.5 0.2 fusion.18
  44.8 0.1 collective-permute-start.2
  44.9 10.5 %collective-permute-done.2 = f32[128,512]{1,0:T(8,128)S(1)} collective-permute-done((f32[128,512]{1,0:T(8,128)S(1)}, f32[128,512]{1,0:T(8,128)S(1)}, u32[]{:S(2)}, u32[]{:S(2)}) %collective-permute-start.2) | collective-permute-done | bytes 262176 | tf_op jit(solution)/shard_map/while/body/eval_jaxpr/ppermute | solution.py:9
  55.3 0.0 collective-permute-start.3
  57.9 30.7 %psum.7 = f32[1]{0:T(128)} all-reduce(f32[1]{0:T(128)} %bitcast), channel_id=1, replica_groups=mesh['groups'=2,'blk'=4,'pair'=2,'sub'=2] {'blk','pair','sub'}, use_global_device_ids=true, to_apply=%region_15.0 | all-reduce | flops 1 | bytes 8 | tf_op jit(solution)/shard_map/psum | solution.py:80
  88.6 0.0 collective-permute-done.3
  88.6 0.0 reduce-scatter.2.cloned.1.call-done
  88.6 1.7 %add.111 = f32[128,512]{1,0:T(8,128)} add(f32[128,512]{1,0:T(8,128)} %reduce-scatter.2.cloned.1.call-done, f32[128,512]{1,0:T(8,128)S(1)} %collective-permute-done.3) | non-fusion elementwise | flops 65536 | bytes 786432 | tf_op jit(solution)/shard_map/add | solution.py:81
Async XLA Ops:
  7.2 10.5 %copy-start = (bf16[128,512]{1,0:T(8,128)(2,1)S(1)}, bf16[128,512]{1,0:T(8,128)(2,1)}, u32[]{:S(2)}) copy-start(bf16[128,512]{1,0:T(8,128)(2,1)} %param.2) | copy-start | bytes 393220
  7.2 81.4 %reduce-scatter.2.cloned.1.call-start = ((), (), s32[]{:S(2)}) async-start(), calls=%async_computation.1 | async-start | bytes 1310720 | tf_op jit(solution)/shard_map/reduce_scatter | solution.py:79
  7.2 27.2 %collective-permute-start = (bf16[128,512]{1,0:T(8,128)(2,1)}, bf16[128,512]{1,0:T(8,128)(2,1)S(1)}, u32[]{:S(2)}, u32[]{:S(2)}) collective-permute-start(bf16[128,512]{1,0:T(8,128)(2,1)} %param.2), channel_id=1, source_target_pairs={{0,4},{4,8},{8,12},{12,0},{1,5},{5,9},{9,13},{13,1},{2,6},{6,10},{... | collective-permute-start | bytes 393224 | tf_op jit(solution)/shard_map/while/body/eval_jaxpr/ppermute | solution.py:9
  17.7 0.7 copy-start.1
  34.4 6.8 %collective-permute-start.1 = (bf16[128,512]{1,0:T(8,128)(2,1)S(1)}, bf16[128,512]{1,0:T(8,128)(2,1)S(1)}, u32[]{:S(2)}, u32[]{:S(2)}) collective-permute-start(bf16[128,512]{1,0:T(8,128)(2,1)S(1)} %collective-permute-done), channel_id=1, source_target_pairs={{0,4},{4,8},{8,12},{12,0},{1,5},{5,9},{9,13},{13,1},{2,6},{6,10},{... | collective-permute-start | bytes 393224 | tf_op jit(solution)/shard_map/ppermute | solution.py:9
  44.8 10.5 %collective-permute-start.2 = (f32[128,512]{1,0:T(8,128)S(1)}, f32[128,512]{1,0:T(8,128)S(1)}, u32[]{:S(2)}, u32[]{:S(2)}) collective-permute-start(f32[128,512]{1,0:T(8,128)S(1)} %fusion.18), channel_id=1, source_target_pairs={{0,4},{4,8},{8,12},{12,0},{1,5},{5,9},{9,13},{13,1},{2,6},{6,10},{... | collective-permute-start | bytes 786440 | tf_op jit(solution)/shard_map/while/body/eval_jaxpr/ppermute | solution.py:9
  55.3 33.3 %collective-permute-start.3 = (f32[128,512]{1,0:T(8,128)S(1)}, f32[128,512]{1,0:T(8,128)S(1)}, u32[]{:S(2)}, u32[]{:S(2)}) collective-permute-start(f32[128,512]{1,0:T(8,128)S(1)} %collective-permute-done.2), channel_id=1, source_target_pairs={{0,8},{4,12},{8,0},{12,4},{1,9},{5,13},{9,1},{13,5},{2,10},{6,14},... | collective-permute-start | bytes 786440 | tf_op jit(solution)/shard_map/ppermute | solution.py:9
Sparse Core Ops, SparseCore 0:
  44.7 22.5 reduce-scatter.1
where the time goes:
time: 97.5 us; the launch traced here: 97.1 us
  blocking collectives  51.4 us (53%)
  waiting for transfers between devices  16.6 us (17%)
  between operations  16.6 us (17%)
  matrix products  6.17 us (6%)
  starting transfers between devices  3.4 us (3%)
  other arithmetic  2.31 us (2%)
    psum x1, blocking collectives, shards(): total_loss = lax.psum(loss_part, ('blk', 'pair', 'sub'))  30.7 us
    ppermute x4, waiting for transfers between devices, passed_along(): lax.ppermute(shard, axis, [(i, (i + by) % size) for i in range(size)])  16.5 us
    all_gather x1, blocking collectives, shards(): piece = lax.all_gather(real, 'blk', axis=0, tiled=True)  13.3 us
    all_gather x1, blocking collectives, shards(): home = lax.all_gather(generated, ('pair', 'sub'), axis=0, tiled=True)  7.37 us
    dot_general x4, matrix products, pair_dist(): lax.dot_general(home, other, (((1,), (1,)), ((), ())), preferred_element_...  3.44 us
    ppermute x4, starting transfers between devices, passed_along(): lax.ppermute(shard, axis, [(i, (i + by) % size) for i in range(size)])  3.36 us
    dot_general x4, matrix products, home_term(): jnp.dot(weight.astype(jnp.bfloat16), other, preferred_element_type=jnp.fl...  2.49 us
  transfers between devices with their start and end apart: 5, of which 2 were waited for; matrix products, arithmetic and copies ran while one was open for 4% of the time, Pallas kernels for 0%

commit v1 on v0

--- a/solution.py
+++ b/solution.py
@@ -1,7 +1,152 @@
+import functools
+
 import jax
 import jax.numpy as jnp
 from jax import lax
+from jax.experimental import pallas as pl
+from jax.experimental.pallas import tpu as pltpu
 from jax.sharding import PartitionSpec as P
+
+AXES = ("blk", "pair", "sub")
+EVEN_ORDER = (("pair", 1), ("blk", 2), ("blk", 1))
+ODD_ORDER = (("blk", 2), ("blk", 1), ("pair", 1))
+CHIP = (("sub", 1),)
+
+
+def swap_pairs(sizes, even_moves, odd_moves):
+    blk, pair, sub = sizes
+    pairs = []
+    for z in range(blk):
+        for x in range(pair):
+            for s in range(sub):
+                at = {"blk": z, "pair": x, "sub": s}
+                for axis, flip in odd_moves if s else even_moves:
+                    at[axis] ^= flip
+                source = (z * pair + x) * sub + s
+                target = (at["blk"] * pair + at["pair"]) * sub + at["sub"]
+                pairs.append((source, target))
+    return pairs
+
+
+def swapped(block, sizes, even_moves, odd_moves):
+    return lax.ppermute(block, AXES, swap_pairs(sizes, even_moves, odd_moves))
+
+
+def gathered_blocks(own, sizes):
+    def step(block, index):
+        return swapped(block, sizes, EVEN_ORDER[index : index + 1], ODD_ORDER[index : index + 1])
+
+    first = step(own, 0)
+    second = step(own, 1)
+    third = step(own, 2)
+    first_second = step(first, 1)
+    first_third = step(first, 2)
+    second_third = step(second, 2)
+    all_three = step(first_second, 2)
+    lane = [own, first, second, third, first_second, first_third, second_third, all_three]
+    return [(block, swapped(block, sizes, CHIP, CHIP)) for block in lane]
+
+
+def whole_kernel(g_rows, ratio, inv_total, *refs):
+    n_blocks = len(refs) - 6
+    blocks = refs[:n_blocks]
+    grad_ref, loss_ref, ws, ncol, nrow, pulled = refs[n_blocks:]
+    width = ws.shape[1]
+    r_rows = blocks[0].shape[0] - g_rows
+    gens = g_rows * n_blocks
+    tile = 2 * g_rows
+    scale = jnp.asarray(-2.0 / width, jnp.bfloat16)
+    eye = lax.broadcasted_iota(jnp.int32, (g_rows, g_rows), 0) == lax.broadcasted_iota(
+        jnp.int32, (g_rows, g_rows), 1
+    )
+
+    def put_norms(row, count, value):
+        v = value.astype(jnp.float32)
+        n = jnp.sum(v * v, axis=1, keepdims=True) * (1.0 / width) + 0.5
+        ncol[pl.ds(row, count), :] = jnp.broadcast_to(n, (count, 128))
+
+    for i, block in enumerate(blocks):
+        g = block[0:g_rows, :]
+        r = block[g_rows : g_rows + r_rows, :]
+        ws[i * g_rows : (i + 1) * g_rows, :] = g
+        ws[gens + i * r_rows : gens + (i + 1) * r_rows, :] = r
+        put_norms(i * g_rows, g_rows, g)
+        put_norms(gens + i * r_rows, r_rows, r)
+    for i in range(ws.shape[0] // g_rows):
+        n = ncol[i * g_rows : (i + 1) * g_rows, :]
+        row = jnp.sum(jnp.where(eye, n, 0.0), axis=0, keepdims=True)
+        q, half = divmod(i, 2)
+        nrow[q, :, half * g_rows : (half + 1) * g_rows] = jnp.broadcast_to(row, (8, g_rows))
+
+    own = ws[0:g_rows, :] * scale
+    own_n = ncol[0:g_rows, :]
+    pulled[...] = jnp.zeros_like(pulled)
+
+    def spread_of(lhs, lhs_n, q):
+        rhs = ws[pl.ds(pl.multiple_of(q * tile, tile), tile), :]
+        c = lax.dot_general(lhs, rhs, (((1,), (1,)), ((), ())), preferred_element_type=jnp.float32)
+        n = jnp.concatenate([lhs_n, lhs_n], axis=1)
+        rows = c.shape[0]
+        nr = nrow[q]
+        nr = jnp.broadcast_to(nr[None], (rows // 8, 8, tile)).reshape(rows, tile)
+        return jnp.maximum((n + nr) + c, 1.0)
+
+    def own_step(q, carry):
+        w = lax.rsqrt(spread_of(own, own_n, q))
+        sign = jnp.where(q * tile < gens, 1.0, -ratio)
+        w = w * sign
+        rhs = ws[pl.ds(pl.multiple_of(q * tile, tile), tile), :]
+        pulled[...] += jnp.dot(w.astype(jnp.bfloat16), rhs, preferred_element_type=jnp.float32)
+        return carry + w[:, 0:128] + w[:, 128:256]
+
+    w_sum = lax.fori_loop(0, ws.shape[0] // tile, own_step, jnp.zeros((g_rows, 128), jnp.float32))
+    w_sum = jnp.sum(w_sum, axis=1, keepdims=True)
+    grad_ref[...] = (pulled[...] - ws[0:g_rows, :].astype(jnp.float32) * w_sum) * inv_total
+
+    def tile_sum(p, q):
+        at = pl.ds(pl.multiple_of(p * tile, tile), tile)
+        s = spread_of(ws[at, :] * scale, ncol[at, :], q)
+        d = s * lax.rsqrt(s)
+        return jnp.sum(d.reshape(tile // 8, 8, tile), axis=0)
+
+    def column(q, acc):
+        def row(p, acc):
+            return acc + tile_sum(p, q) * jnp.where(p == q, -1.0, -2.0)
+
+        acc = lax.fori_loop(0, q + 1, row, acc)
+        return acc + tile_sum(gens // tile, q) * (2.0 * ratio)
+
+    acc = lax.fori_loop(0, gens // tile, column, jnp.zeros((8, tile), jnp.float32))
+    loss_ref[0] = jnp.sum(acc) * (inv_total * inv_total)
+
+
+def small_shards(sizes, generated, real):
+    g_rows, width = generated.shape
+    r_rows = real.shape[0]
+    own = jnp.concatenate([generated, real], axis=0)
+    blocks = [block for both in gathered_blocks(own, sizes) for block in both]
+    n = len(blocks)
+    total = g_rows * n
+    rows = (g_rows + r_rows) * n
+    kernel = functools.partial(whole_kernel, g_rows, float(g_rows / r_rows), 1.0 / total)
+    vmem = pl.BlockSpec(memory_space=pltpu.VMEM)
+    grad, loss = pl.pallas_call(
+        kernel,
+        out_shape=(
+            jax.ShapeDtypeStruct((g_rows, width), jnp.float32),
+            jax.ShapeDtypeStruct((1,), jnp.float32),
+        ),
+        in_specs=[vmem] * n,
+        out_specs=(vmem, pl.BlockSpec(memory_space=pltpu.SMEM)),
+        scratch_shapes=[
+            pltpu.VMEM((rows, width), jnp.bfloat16),
+            pltpu.VMEM((rows, 128), jnp.float32),
+            pltpu.VMEM((rows // (2 * g_rows), 8, 2 * g_rows), jnp.float32),
+            pltpu.VMEM((g_rows, width), jnp.float32),
+        ],
+        compiler_params=pltpu.CompilerParams(vmem_limit_bytes=32 * 1024 * 1024),
+    )(*blocks)
+    return grad, loss
 
 
 def passed_along(shard, axis, by):
@@ -34,7 +179,7 @@
     return factor * (other.astype(jnp.float32) * jnp.sum(weight, axis=0)[:, None] - pulled)
 
 
-def shards(generated, real):
+def large_shards(generated, real):
     cycle_size = lax.axis_size("blk")
     half_way = cycle_size // 2
     devices_all = lax.axis_size(("blk", "pair", "sub"))
@@ -82,6 +227,8 @@
 
 
 def solution(mesh):
+    sizes = tuple(mesh.shape[axis] for axis in AXES)
+    shards = functools.partial(small_shards, sizes) if sizes == (4, 2, 2) else large_shards
     in_specs = (
         P(("groups", "blk", "pair", "sub"), None),
         P(("groups", "blk", "pair", "sub"), None),

time: 97.5 us -> 41.3 us (0.42)
  blocking collectives: 51.4 us -> 0 us
  Pallas kernels: 0 us -> 17.6 us
  between operations: 16.6 us -> 0.69 us
  starting transfers between devices: 3.4 us -> 13.2 us
  waiting for transfers between devices: 16.6 us -> 8.43 us
  matrix products: 6.17 us -> 0 us
  other arithmetic: 2.31 us -> 0 us
    psum x1 -> x0, blocking collectives: 30.7 us -> none  [shards(): total_loss = lax.psum(loss_part, ('blk', 'pair', 'sub'))]
    all_gather x2 -> x0, blocking collectives: 20.7 us -> none  [the longest x1 13.3 us: shards(): piece = lax.all_gather(real, 'blk', axis=0, tiled=True)]
    pallas_call x0 -> x1, Pallas kernels: none -> 17.6 us  [small_shards(): pl.pallas_call(kernel, out_shape=(jax.ShapeDtypeStruct((g_rows, width), j...]
    ppermute x4 -> x15, starting transfers between devices: 3.36 us -> 13.2 us  [swapped(): return lax.ppermute(block, AXES, swap_pairs(sizes, even_moves, odd_moves))]
    ppermute x4 -> x15, waiting for transfers between devices: 16.5 us -> 8.43 us  [swapped(): return lax.ppermute(block, AXES, swap_pairs(sizes, even_moves, odd_moves))]
    dot_general x9 -> x0, matrix products: 6.17 us -> none  [the longest x4 3.44 us: pair_dist(): lax.dot_general(home, other, (((1,), (1,)), ((), ())), preferred_element_...]
    add x1 -> x0, other arithmetic: 1.69 us -> none  [shards(): return (own_rows + partner, total_loss.reshape(1))]
  transfers between devices with their start and end apart: 5 -> 15, of which waited for: 2 -> 7; matrix products, arithmetic and copies ran while one was open for 4% -> 0% of each run, Pallas kernels for 0% -> 0%
where the time goes in v1:
time: 41.3 us; the launch traced here: 40.8 us
  Pallas kernels  17.6 us (43%)
  starting transfers between devices  13.2 us (32%)
  waiting for transfers between devices  8.43 us (20%)
  local copies, waits for them, and re-layouts  0.93 us (2%)
  between operations  0.69 us (2%)
    pallas_call x1, Pallas kernels, small_shards(): pl.pallas_call(kernel, out_shape=(jax.ShapeDtypeStruct((g_rows, width), j...  17.6 us
    ppermute x15, starting transfers between devices, swapped(): return lax.ppermute(block, AXES, swap_pairs(sizes, even_moves, odd_moves))  13.2 us
    ppermute x15, waiting for transfers between devices, swapped(): return lax.ppermute(block, AXES, swap_pairs(sizes, even_moves, odd_moves))  8.43 us
    unnamed x3, local copies, waits for them, and re-layouts  0.92 us
  transfers between devices with their start and end apart: 15, of which 7 were waited for; matrix products, arithmetic and copies ran while one was open for 0% of the time, Pallas kernels for 0%

profile of v1, /device:TPU:0, one launch (start us, length us, event | category | flops | bytes accessed | tf_op | source)
XLA Modules:
  0.0 40.8 jit_solution(10769844186103233956)
XLA Ops:
  0.6 0.0 copy-start
  0.6 0.9 %constant_dynamic-update-slice_fusion.1 = bf16[144,512]{1,0:T(8,128)(2,1)S(1)} fusion(bf16[128,512]{1,0:T(8,128)(2,1)} %param.2), kind=kLoop, calls=%fused_computation.1 | loop fusion | bytes 262144
  1.6 0.0 copy-done
  1.6 3.0 %collective-permute-start.1 = (bf16[144,512]{1,0:T(8,128)(2,1)S(1)}, bf16[144,512]{1,0:T(8,128)(2,1)S(1)}, u32[]{:S(2)}, u32[]{:S(2)}) collective-permute-start(bf16[144,512]{1,0:T(8,128)(2,1)S(1)} %constant_dynamic-update-slice_fusion.refs_0_), channel_id=1, source_target_pairs={{0,2},{1,9},{2,0},{3,11},{4,6},{5,13},{6,4},{7,15},{8,10},{9,1},{1... | collective-permute-start | bytes 442376 | tf_op jit(solution)/shard_map/ppermute | solution.py:32
  4.6 1.6 %collective-permute-start.5 = (bf16[144,512]{1,0:T(8,128)(2,1)S(1)}, bf16[144,512]{1,0:T(8,128)(2,1)S(1)}, u32[]{:S(2)}, u32[]{:S(2)}) collective-permute-start(bf16[144,512]{1,0:T(8,128)(2,1)S(1)} %constant_dynamic-update-slice_fusion.refs_0_), channel_id=1, source_target_pairs={{0,4},{1,3},{2,6},{3,1},{4,0},{5,7},{6,2},{7,5},{8,12},{9,11},{10,... | collective-permute-start | bytes 442376 | tf_op jit(solution)/shard_map/ppermute | solution.py:32
  6.2 2.6 %collective-permute-start.3 = (bf16[144,512]{1,0:T(8,128)(2,1)S(1)}, bf16[144,512]{1,0:T(8,128)(2,1)S(1)}, u32[]{:S(2)}, u32[]{:S(2)}) collective-permute-start(bf16[144,512]{1,0:T(8,128)(2,1)S(1)} %constant_dynamic-update-slice_fusion.refs_0_), channel_id=1, source_target_pairs={{0,8},{1,5},{2,10},{3,7},{4,12},{5,1},{6,14},{7,3},{8,0},{9,13},{1... | collective-permute-start | bytes 442376 | tf_op jit(solution)/shard_map/ppermute | solution.py:32
  8.8 0.0 collective-permute-start
  8.8 0.0 collective-permute-done.1.refs_2_
  8.8 2.6 %collective-permute-start.7 = (bf16[144,512]{1,0:T(8,128)(2,1)S(1)}, bf16[144,512]{1,0:T(8,128)(2,1)S(1)}, u32[]{:S(2)}, u32[]{:S(2)}) collective-permute-start(bf16[144,512]{1,0:T(8,128)(2,1)S(1)} %collective-permute-done.1.refs_2_), channel_id=1, source_target_pairs={{0,8},{1,5},{2,10},{3,7},{4,12},{5,1},{6,14},{7,3},{8,0},{9,13},{1... | collective-permute-start | bytes 442376 | tf_op jit(solution)/shard_map/ppermute | solution.py:32
  11.4 1.1 %collective-permute-done.5.refs_6_ = bf16[144,512]{1,0:T(8,128)(2,1)S(1)} collective-permute-done((bf16[144,512]{1,0:T(8,128)(2,1)S(1)}, bf16[144,512]{1,0:T(8,128)(2,1)S(1)}, u32[]{:S(2)}, u32[]{:S(2)}) %collective-permute-start.5) | collective-permute-done | bytes 147488 | tf_op jit(solution)/shard_map/ppermute | solution.py:32
  12.4 0.0 collective-permute-start.6
  12.4 0.6 %collective-permute-done.3.refs_4_ = bf16[144,512]{1,0:T(8,128)(2,1)S(1)} collective-permute-done((bf16[144,512]{1,0:T(8,128)(2,1)S(1)}, bf16[144,512]{1,0:T(8,128)(2,1)S(1)}, u32[]{:S(2)}, u32[]{:S(2)}) %collective-permute-start.3) | collective-permute-done | bytes 147488 | tf_op jit(solution)/shard_map/ppermute | solution.py:32
  13.1 1.4 %collective-permute-start.11 = (bf16[144,512]{1,0:T(8,128)(2,1)S(1)}, bf16[144,512]{1,0:T(8,128)(2,1)S(1)}, u32[]{:S(2)}, u32[]{:S(2)}) collective-permute-start(bf16[144,512]{1,0:T(8,128)(2,1)S(1)} %collective-permute-done.3.refs_4_), channel_id=1, source_target_pairs={{0,4},{1,3},{2,6},{3,1},{4,0},{5,7},{6,2},{7,5},{8,12},{9,11},{10,... | collective-permute-start | bytes 442376 | tf_op jit(solution)/shard_map/ppermute | solution.py:32
  14.5 0.0 collective-permute-start.4
  14.5 0.0 collective-permute-done.refs_1_
  14.5 0.7 %collective-permute-start.9 = (bf16[144,512]{1,0:T(8,128)(2,1)S(1)}, bf16[144,512]{1,0:T(8,128)(2,1)S(1)}, u32[]{:S(2)}, u32[]{:S(2)}) collective-permute-start(bf16[144,512]{1,0:T(8,128)(2,1)S(1)} %collective-permute-done.1.refs_2_), channel_id=1, source_target_pairs={{0,4},{1,3},{2,6},{3,1},{4,0},{5,7},{6,2},{7,5},{8,12},{9,11},{10,... | collective-permute-start | bytes 442376 | tf_op jit(solution)/shard_map/ppermute | solution.py:32
  15.2 1.6 %collective-permute-done.7.refs_8_ = bf16[144,512]{1,0:T(8,128)(2,1)S(1)} collective-permute-done((bf16[144,512]{1,0:T(8,128)(2,1)S(1)}, bf16[144,512]{1,0:T(8,128)(2,1)S(1)}, u32[]{:S(2)}, u32[]{:S(2)}) %collective-permute-start.7) | collective-permute-done | bytes 147488 | tf_op jit(solution)/shard_map/ppermute | solution.py:32
  16.7 0.8 %collective-permute-start.13 = (bf16[144,512]{1,0:T(8,128)(2,1)S(1)}, bf16[144,512]{1,0:T(8,128)(2,1)S(1)}, u32[]{:S(2)}, u32[]{:S(2)}) collective-permute-start(bf16[144,512]{1,0:T(8,128)(2,1)S(1)} %collective-permute-done.7.refs_8_), channel_id=1, source_target_pairs={{0,4},{1,3},{2,6},{3,1},{4,0},{5,7},{6,2},{7,5},{8,12},{9,11},{10,... | collective-permute-start | bytes 442376 | tf_op jit(solution)/shard_map/ppermute | solution.py:32
  17.6 0.0 collective-permute-done.6.refs_7_
  17.6 0.0 collective-permute-start.2
  17.6 0.7 %collective-permute-done.11.refs_12_ = bf16[144,512]{1,0:T(8,128)(2,1)S(1)} collective-permute-done((bf16[144,512]{1,0:T(8,128)(2,1)S(1)}, bf16[144,512]{1,0:T(8,128)(2,1)S(1)}, u32[]{:S(2)}, u32[]{:S(2)}) %collective-permute-start.11) | collective-permute-done | bytes 147488 | tf_op jit(solution)/shard_map/ppermute | solution.py:32
  18.3 0.0 collective-permute-start.8
  18.3 0.0 collective-permute-done.4.refs_5_
  18.3 0.5 %collective-permute-start.12 = (bf16[144,512]{1,0:T(8,128)(2,1)S(1)}, bf16[144,512]{1,0:T(8,128)(2,1)S(1)}, u32[]{:S(2)}, u32[]{:S(2)}) collective-permute-start(bf16[144,512]{1,0:T(8,128)(2,1)S(1)} %collective-permute-done.11.refs_12_), channel_id=1, source_target_pairs={{0,1},{1,0},{2,3},{3,2},{4,5},{5,4},{6,7},{7,6},{8,9},{9,8},{10,11... | collective-permute-start | bytes 442376 | tf_op jit(solution)/shard_map/ppermute | solution.py:32
  18.8 1.1 %collective-permute-done.9.refs_10_ = bf16[144,512]{1,0:T(8,128)(2,1)S(1)} collective-permute-done((bf16[144,512]{1,0:T(8,128)(2,1)S(1)}, bf16[144,512]{1,0:T(8,128)(2,1)S(1)}, u32[]{:S(2)}, u32[]{:S(2)}) %collective-permute-start.9) | collective-permute-done | bytes 147488 | tf_op jit(solution)/shard_map/ppermute | solution.py:32
  19.8 0.0 collective-permute-start.10
  19.8 2.0 %collective-permute-done.13.refs_14_ = bf16[144,512]{1,0:T(8,128)(2,1)S(1)} collective-permute-done((bf16[144,512]{1,0:T(8,128)(2,1)S(1)}, bf16[144,512]{1,0:T(8,128)(2,1)S(1)}, u32[]{:S(2)}, u32[]{:S(2)}) %collective-permute-start.13) | collective-permute-done | bytes 147488 | tf_op jit(solution)/shard_map/ppermute | solution.py:32
  21.9 0.0 collective-permute-start.14
  21.9 0.0 collective-permute-done.2.refs_3_
  21.9 0.0 collective-permute-done.12.refs_13_
  21.9 0.0 collective-permute-done.10.refs_11_
  21.9 0.0 collective-permute-done.8.refs_9_
  21.9 1.3 %collective-permute-done.14.refs_15_ = bf16[144,512]{1,0:T(8,128)(2,1)S(1)} collective-permute-done((bf16[144,512]{1,0:T(8,128)(2,1)S(1)}, bf16[144,512]{1,0:T(8,128)(2,1)S(1)}, u32[]{:S(2)}, u32[]{:S(2)}) %collective-permute-start.14) | collective-permute-done | bytes 147488 | tf_op jit(solution)/shard_map/ppermute | solution.py:32
  23.3 17.6 %shard_map.41 = (f32[128,512]{1,0:T(8,128)}, f32[1]{0:T(128)}) custom-call(bf16[144,512]{1,0:T(8,128)(2,1)S(1)} %constant_dynamic-update-slice_fusion.refs_0_, bf16[144,512]{1,0:T(8,128)(2,1)S(1)} %collective-permute-done.refs_1_, bf16[144,512]{1,0:T(8,128)(2,1)S(1)} %collective-permute-done.1.refs_2_, bf16[144,512]{1,0:T(8,128)(2,1)S(1)} %collective-permute-done.2.refs_3_, ...), custom_call_target="tpu_custom_call" | custom-call | tf_op jit(solution)/shard_map/pallas_call | solution.py:133
  (1 shorter events, 0.0 us)
Async XLA Ops:
  0.6 0.9 %copy-start = (bf16[16,512]{1,0:T(8,128)(2,1)S(1)}, bf16[16,512]{1,0:T(8,128)(2,1)}, u32[]{:S(2)}) copy-start(bf16[16,512]{1,0:T(8,128)(2,1)} %param.3) | copy-start | bytes 49156
  1.6 7.2 %collective-permute-start.1 = (bf16[144,512]{1,0:T(8,128)(2,1)S(1)}, bf16[144,512]{1,0:T(8,128)(2,1)S(1)}, u32[]{:S(2)}, u32[]{:S(2)}) collective-permute-start(bf16[144,512]{1,0:T(8,128)(2,1)S(1)} %constant_dynamic-update-slice_fusion.refs_0_), channel_id=1, source_target_pairs={{0,2},{1,9},{2,0},{3,11},{4,6},{5,13},{6,4},{7,15},{8,10},{9,1},{1... | collective-permute-start | bytes 442376 | tf_op jit(solution)/shard_map/ppermute | solution.py:32
  4.6 7.8 %collective-permute-start.5 = (bf16[144,512]{1,0:T(8,128)(2,1)S(1)}, bf16[144,512]{1,0:T(8,128)(2,1)S(1)}, u32[]{:S(2)}, u32[]{:S(2)}) collective-permute-start(bf16[144,512]{1,0:T(8,128)(2,1)S(1)} %constant_dynamic-update-slice_fusion.refs_0_), channel_id=1, source_target_pairs={{0,4},{1,3},{2,6},{3,1},{4,0},{5,7},{6,2},{7,5},{8,12},{9,11},{10,... | collective-permute-start | bytes 442376 | tf_op jit(solution)/shard_map/ppermute | solution.py:32
  6.2 6.9 %collective-permute-start.3 = (bf16[144,512]{1,0:T(8,128)(2,1)S(1)}, bf16[144,512]{1,0:T(8,128)(2,1)S(1)}, u32[]{:S(2)}, u32[]{:S(2)}) collective-permute-start(bf16[144,512]{1,0:T(8,128)(2,1)S(1)} %constant_dynamic-update-slice_fusion.refs_0_), channel_id=1, source_target_pairs={{0,8},{1,5},{2,10},{3,7},{4,12},{5,1},{6,14},{7,3},{8,0},{9,13},{1... | collective-permute-start | bytes 442376 | tf_op jit(solution)/shard_map/ppermute | solution.py:32
  8.8 5.7 %collective-permute-start = (bf16[144,512]{1,0:T(8,128)(2,1)S(1)}, bf16[144,512]{1,0:T(8,128)(2,1)S(1)}, u32[]{:S(2)}, u32[]{:S(2)}) collective-permute-start(bf16[144,512]{1,0:T(8,128)(2,1)S(1)} %constant_dynamic-update-slice_fusion.refs_0_), channel_id=1, source_target_pairs={{0,1},{1,0},{2,3},{3,2},{4,5},{5,4},{6,7},{7,6},{8,9},{9,8},{10,11... | collective-permute-start | bytes 442376 | tf_op jit(solution)/shard_map/ppermute | solution.py:32
  8.8 8.0 %collective-permute-start.7 = (bf16[144,512]{1,0:T(8,128)(2,1)S(1)}, bf16[144,512]{1,0:T(8,128)(2,1)S(1)}, u32[]{:S(2)}, u32[]{:S(2)}) collective-permute-start(bf16[144,512]{1,0:T(8,128)(2,1)S(1)} %collective-permute-done.1.refs_2_), channel_id=1, source_target_pairs={{0,8},{1,5},{2,10},{3,7},{4,12},{5,1},{6,14},{7,3},{8,0},{9,13},{1... | collective-permute-start | bytes 442376 | tf_op jit(solution)/shard_map/ppermute | solution.py:32
  12.4 5.1 %collective-permute-start.6 = (bf16[144,512]{1,0:T(8,128)(2,1)S(1)}, bf16[144,512]{1,0:T(8,128)(2,1)S(1)}, u32[]{:S(2)}, u32[]{:S(2)}) collective-permute-start(bf16[144,512]{1,0:T(8,128)(2,1)S(1)} %collective-permute-done.5.refs_6_), channel_id=1, source_target_pairs={{0,1},{1,0},{2,3},{3,2},{4,5},{5,4},{6,7},{7,6},{8,9},{9,8},{10,11... | collective-permute-start | bytes 442376 | tf_op jit(solution)/shard_map/ppermute | solution.py:32
  13.1 5.2 %collective-permute-start.11 = (bf16[144,512]{1,0:T(8,128)(2,1)S(1)}, bf16[144,512]{1,0:T(8,128)(2,1)S(1)}, u32[]{:S(2)}, u32[]{:S(2)}) collective-permute-start(bf16[144,512]{1,0:T(8,128)(2,1)S(1)} %collective-permute-done.3.refs_4_), channel_id=1, source_target_pairs={{0,4},{1,3},{2,6},{3,1},{4,0},{5,7},{6,2},{7,5},{8,12},{9,11},{10,... | collective-permute-start | bytes 442376 | tf_op jit(solution)/shard_map/ppermute | solution.py:32
  14.5 3.8 %collective-permute-start.4 = (bf16[144,512]{1,0:T(8,128)(2,1)S(1)}, bf16[144,512]{1,0:T(8,128)(2,1)S(1)}, u32[]{:S(2)}, u32[]{:S(2)}) collective-permute-start(bf16[144,512]{1,0:T(8,128)(2,1)S(1)} %collective-permute-done.3.refs_4_), channel_id=1, source_target_pairs={{0,1},{1,0},{2,3},{3,2},{4,5},{5,4},{6,7},{7,6},{8,9},{9,8},{10,11... | collective-permute-start | bytes 442376 | tf_op jit(solution)/shard_map/ppermute | solution.py:32
  14.5 5.4 %collective-permute-start.9 = (bf16[144,512]{1,0:T(8,128)(2,1)S(1)}, bf16[144,512]{1,0:T(8,128)(2,1)S(1)}, u32[]{:S(2)}, u32[]{:S(2)}) collective-permute-start(bf16[144,512]{1,0:T(8,128)(2,1)S(1)} %collective-permute-done.1.refs_2_), channel_id=1, source_target_pairs={{0,4},{1,3},{2,6},{3,1},{4,0},{5,7},{6,2},{7,5},{8,12},{9,11},{10,... | collective-permute-start | bytes 442376 | tf_op jit(solution)/shard_map/ppermute | solution.py:32
  16.7 5.1 %collective-permute-start.13 = (bf16[144,512]{1,0:T(8,128)(2,1)S(1)}, bf16[144,512]{1,0:T(8,128)(2,1)S(1)}, u32[]{:S(2)}, u32[]{:S(2)}) collective-permute-start(bf16[144,512]{1,0:T(8,128)(2,1)S(1)} %collective-permute-done.7.refs_8_), channel_id=1, source_target_pairs={{0,4},{1,3},{2,6},{3,1},{4,0},{5,7},{6,2},{7,5},{8,12},{9,11},{10,... | collective-permute-start | bytes 442376 | tf_op jit(solution)/shard_map/ppermute | solution.py:32
  17.6 4.3 %collective-permute-start.2 = (bf16[144,512]{1,0:T(8,128)(2,1)S(1)}, bf16[144,512]{1,0:T(8,128)(2,1)S(1)}, u32[]{:S(2)}, u32[]{:S(2)}) collective-permute-start(bf16[144,512]{1,0:T(8,128)(2,1)S(1)} %collective-permute-done.1.refs_2_), channel_id=1, source_target_pairs={{0,1},{1,0},{2,3},{3,2},{4,5},{5,4},{6,7},{7,6},{8,9},{9,8},{10,11... | collective-permute-start | bytes 442376 | tf_op jit(solution)/shard_map/ppermute | solution.py:32
  18.3 3.6 %collective-permute-start.8 = (bf16[144,512]{1,0:T(8,128)(2,1)S(1)}, bf16[144,512]{1,0:T(8,128)(2,1)S(1)}, u32[]{:S(2)}, u32[]{:S(2)}) collective-permute-start(bf16[144,512]{1,0:T(8,128)(2,1)S(1)} %collective-permute-done.7.refs_8_), channel_id=1, source_target_pairs={{0,1},{1,0},{2,3},{3,2},{4,5},{5,4},{6,7},{7,6},{8,9},{9,8},{10,11... | collective-permute-start | bytes 442376 | tf_op jit(solution)/shard_map/ppermute | solution.py:32
  18.3 3.6 %collective-permute-start.12 = (bf16[144,512]{1,0:T(8,128)(2,1)S(1)}, bf16[144,512]{1,0:T(8,128)(2,1)S(1)}, u32[]{:S(2)}, u32[]{:S(2)}) collective-permute-start(bf16[144,512]{1,0:T(8,128)(2,1)S(1)} %collective-permute-done.11.refs_12_), channel_id=1, source_target_pairs={{0,1},{1,0},{2,3},{3,2},{4,5},{5,4},{6,7},{7,6},{8,9},{9,8},{10,11... | collective-permute-start | bytes 442376 | tf_op jit(solution)/shard_map/ppermute | solution.py:32
  19.8 2.1 %collective-permute-start.10 = (bf16[144,512]{1,0:T(8,128)(2,1)S(1)}, bf16[144,512]{1,0:T(8,128)(2,1)S(1)}, u32[]{:S(2)}, u32[]{:S(2)}) collective-permute-start(bf16[144,512]{1,0:T(8,128)(2,1)S(1)} %collective-permute-done.9.refs_10_), channel_id=1, source_target_pairs={{0,1},{1,0},{2,3},{3,2},{4,5},{5,4},{6,7},{7,6},{8,9},{9,8},{10,11... | collective-permute-start | bytes 442376 | tf_op jit(solution)/shard_map/ppermute | solution.py:32
  21.9 1.4 %collective-permute-start.14 = (bf16[144,512]{1,0:T(8,128)(2,1)S(1)}, bf16[144,512]{1,0:T(8,128)(2,1)S(1)}, u32[]{:S(2)}, u32[]{:S(2)}) collective-permute-start(bf16[144,512]{1,0:T(8,128)(2,1)S(1)} %collective-permute-done.13.refs_14_), channel_id=1, source_target_pairs={{0,1},{1,0},{2,3},{3,2},{4,5},{5,4},{6,7},{7,6},{8,9},{9,8},{10,11... | collective-permute-start | bytes 442376 | tf_op jit(solution)/shard_map/ppermute | solution.py:32

commit v2 on v0

--- a/solution.py
+++ b/solution.py
@@ -1,7 +1,220 @@
+import functools
+
 import jax
 import jax.numpy as jnp
 from jax import lax
+from jax.experimental import pallas as pl
+from jax.experimental.pallas import tpu as pltpu
 from jax.sharding import PartitionSpec as P
+
+AXES = ("blk", "pair", "sub")
+SMALL = (4, 2, 2)
+EVEN_MOVES = ((('pair', 1),), (('blk', 2),), (('blk', 1),))
+ODD_MOVES = ((('blk', 2),), (('blk', 1),), (('pair', 1),))
+CHIP_MOVES = (("sub", 1),)
+SENDS = (('a', 'O', 0), ('b', 'O', 1), ('d', 'O', 2), ('c', 'a', 1), ('e', 'a', 2), ('f', 'b', 2), ('g', 'c', 2))
+STAGES = (('O',), ('a',), ('b',), ('d',), ('c',), ('e',), ('f',), ('g',))
+HELD = {}
+
+
+def swap_pairs(sizes, even_moves, odd_moves):
+    blk, pair, sub = sizes
+    pairs = []
+    for z in range(blk):
+        for x in range(pair):
+            for s in range(sub):
+                at = {"blk": z, "pair": x, "sub": s}
+                for axis, flip in odd_moves if s else even_moves:
+                    at[axis] ^= flip
+                source = (z * pair + x) * sub + s
+                target = (at["blk"] * pair + at["pair"]) * sub + at["sub"]
+                pairs.append((source, target))
+    return pairs
+
+
+def swapped(block, sizes, even_moves, odd_moves):
+    return lax.ppermute(block, AXES, swap_pairs(sizes, even_moves, odd_moves))
+
+
+def joined(held, names):
+    return held[names] if names in held else jnp.concatenate([held[n] for n in names])
+
+
+def stage_call(news, olds, carry, g_rows, n_pairs, final):
+    step = olds[0].shape[0] if olds else news[0].shape[0]
+    width = news[0].shape[1]
+    r_rows = step - g_rows
+    n_new = sum(b.shape[0] // step for b in news) // 2
+    n_old = sum(b.shape[0] // step for b in olds) // 2
+    ratio = g_rows / r_rows
+    inv_total = 1.0 / (g_rows * 2 * n_pairs)
+    tile = 2 * g_rows
+    gens_n, reals_n = n_new * tile, n_new * 2 * r_rows
+    first = not olds
+
+    def lanes_of(n, count, offset):
+        row = lax.broadcasted_iota(jnp.int32, (count, 128), 0)
+        lane = lax.broadcasted_iota(jnp.int32, (count, 128), 1)
+        line = jnp.sum(jnp.where(lane == row + offset, n, 0.0), axis=0, keepdims=True)
+        return jnp.broadcast_to(line, (8, 128))
+
+    def fold(d):
+        rows, lanes = d.shape
+        return jnp.sum(d.reshape(rows // 8, 8, lanes), axis=0)
+
+    def kernel(*refs):
+        refs = list(refs)
+
+        def take(count):
+            taken = []
+            while len(taken) < count:
+                ref = refs.pop(0)
+                taken += [(ref, at) for at in range(0, ref.shape[0], step)]
+            return taken
+
+        def gens_of(block):
+            ref, at = block
+            return ref[at : at + g_rows, :]
+
+        def reals_of(block):
+            ref, at = block
+            return ref[at + g_rows : at + step, :]
+
+        new, old = take(2 * n_new), take(2 * n_old)
+        if not first:
+            pulled_in, sums_in, norms_in = refs.pop(0), refs.pop(0), refs.pop(0)
+        gens = jnp.concatenate([gens_of(b) for b in new], axis=0)
+        reals = jnp.concatenate([reals_of(b) for b in new], axis=0)
+        rows = jnp.concatenate([gens, reals], axis=0)
+        v = rows.astype(jnp.float32)
+        n_col = jnp.sum(v * v, axis=1, keepdims=True) * (1.0 / width) + 0.5
+        n_col = jnp.broadcast_to(n_col, (gens_n + reals_n, 128))
+        blocks_n = [
+            lanes_of(n_col[i * g_rows : (i + 1) * g_rows], g_rows, 0) for i in range(2 * n_new)
+        ]
+        new_n = [jnp.concatenate(blocks_n[2 * i : 2 * i + 2], axis=1) for i in range(n_new)]
+        lhs = rows * jnp.asarray(-2.0 / width, rows.dtype)
+
+        def spread(rhs, n_lane, count):
+            c = lax.dot_general(
+                lhs[0:count], rhs, (((1,), (1,)), ((), ())), preferred_element_type=jnp.float32
+            )
+            lanes = c.shape[1]
+            n_row = jnp.concatenate([n_col[0:count]] * pl.cdiv(lanes, 128), axis=1)[:, 0:lanes]
+            n_lane = jnp.broadcast_to(n_lane[None], (count // 8, 8, lanes)).reshape(count, lanes)
+            return jnp.maximum((n_row + n_lane) + c, 1.0)
+
+        def own_part(w):
+            w = w[:, 0:g_rows]
+            w = jnp.concatenate([w[0:gens_n], w[gens_n:] * (-ratio)], axis=0)
+            sums = lax.dot_general(
+                w.astype(jnp.bfloat16),
+                rows,
+                (((0,), (0,)), ((), ())),
+                preferred_element_type=jnp.float32,
+            )
+            return sums, fold(w)
+
+        loss = jnp.zeros((8, tile), jnp.float32)
+        for i in range(n_old + n_new):
+            if i < n_old:
+                rhs = jnp.concatenate([gens_of(old[2 * i]), gens_of(old[2 * i + 1])], axis=0)
+                s = spread(rhs, norms_in[i], gens_n + reals_n)
+            else:
+                j = i - n_old
+                s = spread(gens[j * tile : (j + 1) * tile], new_n[j], gens_n + reals_n)
+            w = lax.rsqrt(s)
+            if i == 0:
+                pulled, w_sum = own_part(w)
+            d = s * w
+            times = -2.0 if i < n_old else -1.0
+            loss += fold(d[0:gens_n]) * times + fold(d[gens_n:]) * (2.0 * ratio)
+        if not first:
+            old_reals = jnp.concatenate([reals_of(b) for b in old], axis=0)
+            s = spread(old_reals, norms_in[n_pairs][:, 0 : old_reals.shape[0]], gens_n)
+            d = jnp.sum(fold(s * lax.rsqrt(s)), axis=1, keepdims=True) * (2.0 * ratio)
+            lane = lax.broadcasted_iota(jnp.int32, (8, tile), 1)
+            loss += jnp.where(lane == 0, d, 0.0)
+            pulled = pulled + pulled_in[...]
+            w_sum = w_sum + sums_in[0:8, 0:128]
+            loss = loss + sums_in[8:16, :]
+        if final:
+            grad_ref, loss_ref = refs
+            line = jnp.broadcast_to(jnp.sum(w_sum, axis=0, keepdims=True), (g_rows, 128))
+            row = lax.broadcasted_iota(jnp.int32, (g_rows, g_rows), 0)
+            lane = lax.broadcasted_iota(jnp.int32, (g_rows, g_rows), 1)
+            w_col = jnp.sum(jnp.where(row == lane, line, 0.0), axis=1, keepdims=True)
+            own = gens_of(new[0] if first else old[0]).astype(jnp.float32)
+            grad_ref[...] = (pulled - own * w_col) * inv_total
+            loss_ref[0] = jnp.sum(loss) * (inv_total * inv_total)
+        else:
+            pulled_ref, sums_ref, norms_ref = refs
+            pulled_ref[...] = pulled
+            sums_ref[0:8, 0:128] = w_sum
+            sums_ref[8:16, :] = loss
+            for i in range(n_old):
+                norms_ref[i] = norms_in[i]
+            for i in range(n_new):
+                norms_ref[n_old + i] = new_n[i]
+            at = n_old * 2 * r_rows
+            real_n = jnp.concatenate(
+                [lanes_of(n_col[gens_n:], reals_n, at - 128 * half) for half in range(2)], axis=1
+            )
+            norms_ref[n_pairs] = real_n if first else real_n + norms_in[n_pairs]
+
+    vmem = pl.BlockSpec(memory_space=pltpu.VMEM)
+    f32 = functools.partial(jax.ShapeDtypeStruct, dtype=jnp.float32)
+    if final:
+        out_shape = (f32((g_rows, width)), f32((1,)))
+        out_specs = (vmem, pl.BlockSpec(memory_space=pltpu.SMEM))
+    else:
+        out_shape = (f32((g_rows, width)), f32((16, tile)), f32((n_pairs + 1, 8, tile)))
+        out_specs = (vmem,) * 3
+    entries = (gens_n + reals_n) * ((n_old + n_new) * tile + n_old * 2 * r_rows)
+    operands = [*news, *olds, *carry]
+    return pl.pallas_call(
+        kernel,
+        out_shape=out_shape,
+        in_specs=[vmem] * len(operands),
+        out_specs=out_specs,
+        cost_estimate=pl.CostEstimate(
+            flops=int(2 * entries * width * 1), bytes_accessed=1024, transcendentals=entries
+        ),
+        compiler_params=pltpu.CompilerParams(vmem_limit_bytes=32 * 1024 * 1024),
+    )(*operands)
+
+
+def small_shards(sizes, generated, real):
+    own = jnp.concatenate([generated, real], axis=0)
+    g_rows, block_rows = generated.shape[0], own.shape[0]
+    n_pairs = sizes[0] * sizes[1]
+    lane, chip = {"O": own}, {}
+    stages, seen, carry = [], [], ()
+
+    def held_back(name, value):
+        if name not in HELD:
+            return value
+        return lax.optimization_barrier((value, stages[HELD[name]][1]))[0]
+
+    def run_stages():
+        nonlocal seen, carry
+        while len(stages) < len(STAGES) and all(n in lane for n in STAGES[len(stages)]):
+            new = []
+            for n in STAGES[len(stages)]:
+                chip[n] = swapped(held_back("S" + n, lane[n]), sizes, CHIP_MOVES, CHIP_MOVES)
+                new += [lane[n], chip[n]]
+            final = len(stages) == len(STAGES) - 1
+            carry = stage_call(new, seen, carry, g_rows, n_pairs, final)
+            stages.append(carry)
+            seen = seen + new
+
+    run_stages()
+    for name, sources, move in SENDS:
+        block = held_back(name, joined(lane, sources))
+        lane[name] = swapped(block, sizes, EVEN_MOVES[move], ODD_MOVES[move])
+        run_stages()
+    assert sum(b.shape[0] for b in seen) == 2 * n_pairs * block_rows
+    return carry
 
 
 def passed_along(shard, axis, by):
@@ -34,7 +247,7 @@
     return factor * (other.astype(jnp.float32) * jnp.sum(weight, axis=0)[:, None] - pulled)
 
 
-def shards(generated, real):
+def large_shards(generated, real):
     cycle_size = lax.axis_size("blk")
     half_way = cycle_size // 2
     devices_all = lax.axis_size(("blk", "pair", "sub"))
@@ -82,6 +295,8 @@
 
 
 def solution(mesh):
+    sizes = tuple(mesh.shape[axis] for axis in AXES)
+    shards = functools.partial(small_shards, sizes) if sizes == SMALL else large_shards
     in_specs = (
         P(("groups", "blk", "pair", "sub"), None),
         P(("groups", "blk", "pair", "sub"), None),

time: 97.5 us -> 27.6 us (0.28)
  the two profiles are of different devices: /device:TPU:0 before, /device:TPU:25 now
where the time goes in v2:
time: 27.6 us; the launch traced here: 27.5 us
  starting transfers between devices  10.5 us (38%)
  waiting for transfers between devices  8.07 us (29%)
  Pallas kernels  7.27 us (26%)
  local copies, waits for them, and re-layouts  0.93 us (3%)
  between operations  0.73 us (3%)
    ppermute x15, starting transfers between devices, swapped(): return lax.ppermute(block, AXES, swap_pairs(sizes, even_moves, odd_moves))  10.5 us
    ppermute x15, waiting for transfers between devices, swapped(): return lax.ppermute(block, AXES, swap_pairs(sizes, even_moves, odd_moves))  8.07 us
    pallas_call x8, Pallas kernels, stage_call(): pl.pallas_call(kernel, out_shape=out_shape, in_specs=[vmem] * len(operand...  7.27 us
    unnamed x3, local copies, waits for them, and re-layouts  0.92 us
  transfers between devices with their start and end apart: 15, of which 2 were waited for; matrix products, arithmetic and copies ran while one was open for 0% of the time, Pallas kernels for 19%

profile of v2, /device:TPU:25, one launch (start us, length us, event | category | flops | bytes accessed | tf_op | source)
XLA Modules:
  0.0 27.5 jit_solution(18435766257645470952)
XLA Ops:
  0.6 0.0 copy-start
  0.6 0.9 %constant_dynamic-update-slice_fusion.1 = bf16[144,512]{1,0:T(8,128)(2,1)S(1)} fusion(bf16[128,512]{1,0:T(8,128)(2,1)} %param.2), kind=kLoop, calls=%fused_computation.1 | loop fusion | bytes 262144
  1.6 0.0 copy-done
  1.6 0.1 collective-permute-start
  1.7 0.2 collective-permute-start.6
  1.9 2.3 %collective-permute-start.4 = (bf16[144,512]{1,0:T(8,128)(2,1)S(1)}, bf16[144,512]{1,0:T(8,128)(2,1)S(1)}, u32[]{:S(2)}, u32[]{:S(2)}) collective-permute-start(bf16[144,512]{1,0:T(8,128)(2,1)S(1)} %constant_dynamic-update-slice_fusion.refs_0_.refs_2_), channel_id=1, source_target_pairs={{0,1},{1,0},{2,3},{3,2},{4,5},{5,4},{6,7},{7,6},{8,9},{9,8},{10,11... | collective-permute-start | bytes 442376 | tf_op jit(solution)/shard_map/ppermute | solution.py:36
  4.2 0.3 collective-permute-start.8
  4.4 5.9 %collective-permute-done.refs_0_.refs_4_ = bf16[144,512]{1,0:T(8,128)(2,1)S(1)} collective-permute-done((bf16[144,512]{1,0:T(8,128)(2,1)S(1)}, bf16[144,512]{1,0:T(8,128)(2,1)S(1)}, u32[]{:S(2)}, u32[]{:S(2)}) %collective-permute-start) | collective-permute-done | bytes 147488 | tf_op jit(solution)/shard_map/ppermute | solution.py:36
  10.3 0.0 collective-permute-start.1
  10.3 0.0 collective-permute-start.5
  10.3 0.0 collective-permute-done.6.refs_0_.refs_6_
  10.3 1.6 %collective-permute-start.7 = (bf16[144,512]{1,0:T(8,128)(2,1)S(1)}, bf16[144,512]{1,0:T(8,128)(2,1)S(1)}, u32[]{:S(2)}, u32[]{:S(2)}) collective-permute-start(bf16[144,512]{1,0:T(8,128)(2,1)S(1)} %collective-permute-done.6.refs_0_.refs_6_), channel_id=1, source_target_pairs={{0,1},{1,0},{2,3},{3,2},{4,5},{5,4},{6,7},{7,6},{8,9},{9,8},{10,11... | collective-permute-start | bytes 442376 | tf_op jit(solution)/shard_map/ppermute | solution.py:36
  11.9 0.0 collective-permute-done.4.refs_1_.refs_3_
  11.9 1.2 %collective-permute-start.11 = (bf16[144,512]{1,0:T(8,128)(2,1)S(1)}, bf16[144,512]{1,0:T(8,128)(2,1)S(1)}, u32[]{:S(2)}, u32[]{:S(2)}) collective-permute-start(bf16[144,512]{1,0:T(8,128)(2,1)S(1)} %collective-permute-done.refs_0_.refs_4_), channel_id=1, source_target_pairs={{0,4},{1,3},{2,6},{3,1},{4,0},{5,7},{6,2},{7,5},{8,12},{9,11},{10,... | collective-permute-start | bytes 442376 | tf_op jit(solution)/shard_map/ppermute | solution.py:36
  13.1 0.0 collective-permute-done.8.refs_0_.refs_8_
  13.1 0.3 collective-permute-start.13
  13.3 2.2 %collective-permute-done.1.refs_0_.refs_10_ = bf16[144,512]{1,0:T(8,128)(2,1)S(1)} collective-permute-done((bf16[144,512]{1,0:T(8,128)(2,1)S(1)}, bf16[144,512]{1,0:T(8,128)(2,1)S(1)}, u32[]{:S(2)}, u32[]{:S(2)}) %collective-permute-start.1) | collective-permute-done | bytes 147488 | tf_op jit(solution)/shard_map/ppermute | solution.py:36
  15.5 3.4 %collective-permute-start.2 = (bf16[144,512]{1,0:T(8,128)(2,1)S(1)}, bf16[144,512]{1,0:T(8,128)(2,1)S(1)}, u32[]{:S(2)}, u32[]{:S(2)}) collective-permute-start(bf16[144,512]{1,0:T(8,128)(2,1)S(1)} %collective-permute-done.1.refs_0_.refs_10_), channel_id=1, source_target_pairs={{0,4},{1,3},{2,6},{3,1},{4,0},{5,7},{6,2},{7,5},{8,12},{9,11},{10,... | collective-permute-start | bytes 442376 | tf_op jit(solution)/shard_map/ppermute | solution.py:36
  18.9 0.0 collective-permute-done.5.refs_1_.refs_5_
  18.9 0.0 collective-permute-start.9
  18.9 0.0 collective-permute-done.7.refs_1_.refs_7_
  18.9 0.5 %collective-permute-start.10 = (bf16[144,512]{1,0:T(8,128)(2,1)S(1)}, bf16[144,512]{1,0:T(8,128)(2,1)S(1)}, u32[]{:S(2)}, u32[]{:S(2)}) collective-permute-start(bf16[144,512]{1,0:T(8,128)(2,1)S(1)} %collective-permute-done.1.refs_0_.refs_10_), channel_id=1, source_target_pairs={{0,1},{1,0},{2,3},{3,2},{4,5},{5,4},{6,7},{7,6},{8,9},{9,8},{10,11... | collective-permute-start | bytes 442376 | tf_op jit(solution)/shard_map/ppermute | solution.py:36
  19.4 0.0 collective-permute-done.11.refs_0_.refs_12_
  19.4 0.1 collective-permute-start.12
  19.5 0.6 %shard_map.41 = (f32[128,512]{1,0:T(8,128)S(1)}, f32[16,256]{1,0:T(8,128)S(1)}, f32[9,8,256]{2,1,0:T(8,128)S(1)}) custom-call(bf16[144,512]{1,0:T(8,128)(2,1)S(1)} %constant_dynamic-update-slice_fusion.refs_0_.refs_2_, bf16[144,512]{1,0:T(8,128)(2,1)S(1)} %collective-permute-done.4.refs_1_.refs_3_), custom_call_target="tpu_custom_call" | custom-call | flops 75497472 | bytes 1024 | tf_op jit(solution)/shard_map/pallas_call | solution.py:175
  20.1 0.0 collective-permute-done.13.refs_0_.refs_14_
  20.1 0.5 %collective-permute-start.14 = (bf16[144,512]{1,0:T(8,128)(2,1)S(1)}, bf16[144,512]{1,0:T(8,128)(2,1)S(1)}, u32[]{:S(2)}, u32[]{:S(2)}) collective-permute-start(bf16[144,512]{1,0:T(8,128)(2,1)S(1)} %collective-permute-done.13.refs_0_.refs_14_), channel_id=1, source_target_pairs={{0,1},{1,0},{2,3},{3,2},{4,5},{5,4},{6,7},{7,6},{8,9},{9,8},{10,11... | collective-permute-start | bytes 442376 | tf_op jit(solution)/shard_map/ppermute | solution.py:36
  20.6 0.6 %shard_map.42 = (f32[128,512]{1,0:T(8,128)S(1)}, f32[16,256]{1,0:T(8,128)S(1)}, f32[9,8,256]{2,1,0:T(8,128)S(1)}) custom-call(bf16[144,512]{1,0:T(8,128)(2,1)S(1)} %collective-permute-done.refs_0_.refs_4_, bf16[144,512]{1,0:T(8,128)(2,1)S(1)} %collective-permute-done.5.refs_1_.refs_5_, ...), custom_call_target="tpu_custom_call" | custom-call | flops 160432128 | bytes 1024 | tf_op jit(solution)/shard_map/pallas_call | solution.py:175
  21.2 0.7 %shard_map.43 = (f32[128,512]{1,0:T(8,128)S(1)}, f32[16,256]{1,0:T(8,128)S(1)}, f32[9,8,256]{2,1,0:T(8,128)S(1)}) custom-call(bf16[144,512]{1,0:T(8,128)(2,1)S(1)} %collective-permute-done.6.refs_0_.refs_6_, bf16[144,512]{1,0:T(8,128)(2,1)S(1)} %collective-permute-done.7.refs_1_.refs_7_, ...), custom_call_target="tpu_custom_call" | custom-call | flops 245366784 | bytes 1024 | tf_op jit(solution)/shard_map/pallas_call | solution.py:175
  21.9 0.0 collective-permute-done.2.refs_0_
  21.9 0.1 collective-permute-start.3
  22.1 0.0 collective-permute-done.9.refs_1_.refs_9_
  22.1 0.7 %shard_map.44 = (f32[128,512]{1,0:T(8,128)S(1)}, f32[16,256]{1,0:T(8,128)S(1)}, f32[9,8,256]{2,1,0:T(8,128)S(1)}) custom-call(bf16[144,512]{1,0:T(8,128)(2,1)S(1)} %collective-permute-done.8.refs_0_.refs_8_, bf16[144,512]{1,0:T(8,128)(2,1)S(1)} %collective-permute-done.9.refs_1_.refs_9_, ...), custom_call_target="tpu_custom_call" | custom-call | flops 330301440 | bytes 1024 | tf_op jit(solution)/shard_map/pallas_call | solution.py:175
  22.8 0.0 collective-permute-done.10.refs_1_.refs_11_
  22.8 0.8 %shard_map.45 = (f32[128,512]{1,0:T(8,128)S(1)}, f32[16,256]{1,0:T(8,128)S(1)}, f32[9,8,256]{2,1,0:T(8,128)S(1)}) custom-call(bf16[144,512]{1,0:T(8,128)(2,1)S(1)} %collective-permute-done.1.refs_0_.refs_10_, bf16[144,512]{1,0:T(8,128)(2,1)S(1)} %collective-permute-done.10.refs_1_.refs_11_, ...), custom_call_target="tpu_custom_call" | custom-call | flops 415236096 | bytes 1024 | tf_op jit(solution)/shard_map/pallas_call | solution.py:175
  23.6 0.0 collective-permute-done.12.refs_1_.refs_13_
  23.6 0.9 %shard_map.46 = (f32[128,512]{1,0:T(8,128)S(1)}, f32[16,256]{1,0:T(8,128)S(1)}, f32[9,8,256]{2,1,0:T(8,128)S(1)}) custom-call(bf16[144,512]{1,0:T(8,128)(2,1)S(1)} %collective-permute-done.11.refs_0_.refs_12_, bf16[144,512]{1,0:T(8,128)(2,1)S(1)} %collective-permute-done.12.refs_1_.refs_13_, ...), custom_call_target="tpu_custom_call" | custom-call | flops 500170752 | bytes 1024 | tf_op jit(solution)/shard_map/pallas_call | solution.py:175
  24.5 0.0 collective-permute-done.14.refs_1_.refs_15_
  24.5 1.0 %shard_map.47 = (f32[128,512]{1,0:T(8,128)S(1)}, f32[16,256]{1,0:T(8,128)S(1)}, f32[9,8,256]{2,1,0:T(8,128)S(1)}) custom-call(bf16[144,512]{1,0:T(8,128)(2,1)S(1)} %collective-permute-done.13.refs_0_.refs_14_, bf16[144,512]{1,0:T(8,128)(2,1)S(1)} %collective-permute-done.14.refs_1_.refs_15_, ...), custom_call_target="tpu_custom_call" | custom-call | flops 585105408 | bytes 1024 | tf_op jit(solution)/shard_map/pallas_call | solution.py:175
  25.5 0.0 collective-permute-done.3.refs_1_
  25.5 1.9 %shard_map.48 = (f32[128,512]{1,0:T(8,128)}, f32[1]{0:T(128)}) custom-call(bf16[144,512]{1,0:T(8,128)(2,1)S(1)} %collective-permute-done.2.refs_0_, bf16[144,512]{1,0:T(8,128)(2,1)S(1)} %collective-permute-done.3.refs_1_, bf16[144,512]{1,0:T(8,128)(2,1)S(1)} %constant_dynamic-update-slice_fusion.refs_0_.refs_2_, ...), custom_call_target="tpu_custom_call" | custom-call | flops 670040064 | bytes 1024 | tf_op jit(solution)/shard_map/pallas_call | solution.py:175
  (1 shorter events, 0.0 us)
Async XLA Ops:
  0.6 0.9 %copy-start = (bf16[16,512]{1,0:T(8,128)(2,1)S(1)}, bf16[16,512]{1,0:T(8,128)(2,1)}, u32[]{:S(2)}) copy-start(bf16[16,512]{1,0:T(8,128)(2,1)} %param.3) | copy-start | bytes 49156
  1.6 8.7 %collective-permute-start = (bf16[144,512]{1,0:T(8,128)(2,1)S(1)}, bf16[144,512]{1,0:T(8,128)(2,1)S(1)}, u32[]{:S(2)}, u32[]{:S(2)}) collective-permute-start(bf16[144,512]{1,0:T(8,128)(2,1)S(1)} %constant_dynamic-update-slice_fusion.refs_0_.refs_2_), channel_id=1, source_target_pairs={{0,2},{1,9},{2,0},{3,11},{4,6},{5,13},{6,4},{7,15},{8,10},{9,1},{1... | collective-permute-start | bytes 442376 | tf_op jit(solution)/shard_map/ppermute | solution.py:36
  1.7 8.6 %collective-permute-start.6 = (bf16[144,512]{1,0:T(8,128)(2,1)S(1)}, bf16[144,512]{1,0:T(8,128)(2,1)S(1)}, u32[]{:S(2)}, u32[]{:S(2)}) collective-permute-start(bf16[144,512]{1,0:T(8,128)(2,1)S(1)} %constant_dynamic-update-slice_fusion.refs_0_.refs_2_), channel_id=1, source_target_pairs={{0,8},{1,5},{2,10},{3,7},{4,12},{5,1},{6,14},{7,3},{8,0},{9,13},{1... | collective-permute-start | bytes 442376 | tf_op jit(solution)/shard_map/ppermute | solution.py:36
  1.9 10.0 %collective-permute-start.4 = (bf16[144,512]{1,0:T(8,128)(2,1)S(1)}, bf16[144,512]{1,0:T(8,128)(2,1)S(1)}, u32[]{:S(2)}, u32[]{:S(2)}) collective-permute-start(bf16[144,512]{1,0:T(8,128)(2,1)S(1)} %constant_dynamic-update-slice_fusion.refs_0_.refs_2_), channel_id=1, source_target_pairs={{0,1},{1,0},{2,3},{3,2},{4,5},{5,4},{6,7},{7,6},{8,9},{9,8},{10,11... | collective-permute-start | bytes 442376 | tf_op jit(solution)/shard_map/ppermute | solution.py:36
  4.2 8.9 %collective-permute-start.8 = (bf16[144,512]{1,0:T(8,128)(2,1)S(1)}, bf16[144,512]{1,0:T(8,128)(2,1)S(1)}, u32[]{:S(2)}, u32[]{:S(2)}) collective-permute-start(bf16[144,512]{1,0:T(8,128)(2,1)S(1)} %constant_dynamic-update-slice_fusion.refs_0_.refs_2_), channel_id=1, source_target_pairs={{0,4},{1,3},{2,6},{3,1},{4,0},{5,7},{6,2},{7,5},{8,12},{9,11},{10,... | collective-permute-start | bytes 442376 | tf_op jit(solution)/shard_map/ppermute | solution.py:36
  10.3 5.3 %collective-permute-start.1 = (bf16[144,512]{1,0:T(8,128)(2,1)S(1)}, bf16[144,512]{1,0:T(8,128)(2,1)S(1)}, u32[]{:S(2)}, u32[]{:S(2)}) collective-permute-start(bf16[144,512]{1,0:T(8,128)(2,1)S(1)} %collective-permute-done.refs_0_.refs_4_), channel_id=1, source_target_pairs={{0,8},{1,5},{2,10},{3,7},{4,12},{5,1},{6,14},{7,3},{8,0},{9,13},{1... | collective-permute-start | bytes 442376 | tf_op jit(solution)/shard_map/ppermute | solution.py:36
  10.3 8.6 %collective-permute-start.5 = (bf16[144,512]{1,0:T(8,128)(2,1)S(1)}, bf16[144,512]{1,0:T(8,128)(2,1)S(1)}, u32[]{:S(2)}, u32[]{:S(2)}) collective-permute-start(bf16[144,512]{1,0:T(8,128)(2,1)S(1)} %collective-permute-done.refs_0_.refs_4_), channel_id=1, source_target_pairs={{0,1},{1,0},{2,3},{3,2},{4,5},{5,4},{6,7},{7,6},{8,9},{9,8},{10,11... | collective-permute-start | bytes 442376 | tf_op jit(solution)/shard_map/ppermute | solution.py:36
  10.3 8.6 %collective-permute-start.7 = (bf16[144,512]{1,0:T(8,128)(2,1)S(1)}, bf16[144,512]{1,0:T(8,128)(2,1)S(1)}, u32[]{:S(2)}, u32[]{:S(2)}) collective-permute-start(bf16[144,512]{1,0:T(8,128)(2,1)S(1)} %collective-permute-done.6.refs_0_.refs_6_), channel_id=1, source_target_pairs={{0,1},{1,0},{2,3},{3,2},{4,5},{5,4},{6,7},{7,6},{8,9},{9,8},{10,11... | collective-permute-start | bytes 442376 | tf_op jit(solution)/shard_map/ppermute | solution.py:36
  11.9 7.5 %collective-permute-start.11 = (bf16[144,512]{1,0:T(8,128)(2,1)S(1)}, bf16[144,512]{1,0:T(8,128)(2,1)S(1)}, u32[]{:S(2)}, u32[]{:S(2)}) collective-permute-start(bf16[144,512]{1,0:T(8,128)(2,1)S(1)} %collective-permute-done.refs_0_.refs_4_), channel_id=1, source_target_pairs={{0,4},{1,3},{2,6},{3,1},{4,0},{5,7},{6,2},{7,5},{8,12},{9,11},{10,... | collective-permute-start | bytes 442376 | tf_op jit(solution)/shard_map/ppermute | solution.py:36
  13.1 7.0 %collective-permute-start.13 = (bf16[144,512]{1,0:T(8,128)(2,1)S(1)}, bf16[144,512]{1,0:T(8,128)(2,1)S(1)}, u32[]{:S(2)}, u32[]{:S(2)}) collective-permute-start(bf16[144,512]{1,0:T(8,128)(2,1)S(1)} %collective-permute-done.6.refs_0_.refs_6_), channel_id=1, source_target_pairs={{0,4},{1,3},{2,6},{3,1},{4,0},{5,7},{6,2},{7,5},{8,12},{9,11},{10,... | collective-permute-start | bytes 442376 | tf_op jit(solution)/shard_map/ppermute | solution.py:36
  15.5 6.4 %collective-permute-start.2 = (bf16[144,512]{1,0:T(8,128)(2,1)S(1)}, bf16[144,512]{1,0:T(8,128)(2,1)S(1)}, u32[]{:S(2)}, u32[]{:S(2)}) collective-permute-start(bf16[144,512]{1,0:T(8,128)(2,1)S(1)} %collective-permute-done.1.refs_0_.refs_10_), channel_id=1, source_target_pairs={{0,4},{1,3},{2,6},{3,1},{4,0},{5,7},{6,2},{7,5},{8,12},{9,11},{10,... | collective-permute-start | bytes 442376 | tf_op jit(solution)/shard_map/ppermute | solution.py:36
  18.9 3.2 %collective-permute-start.9 = (bf16[144,512]{1,0:T(8,128)(2,1)S(1)}, bf16[144,512]{1,0:T(8,128)(2,1)S(1)}, u32[]{:S(2)}, u32[]{:S(2)}) collective-permute-start(bf16[144,512]{1,0:T(8,128)(2,1)S(1)} %collective-permute-done.8.refs_0_.refs_8_), channel_id=1, source_target_pairs={{0,1},{1,0},{2,3},{3,2},{4,5},{5,4},{6,7},{7,6},{8,9},{9,8},{10,11... | collective-permute-start | bytes 442376 | tf_op jit(solution)/shard_map/ppermute | solution.py:36
  18.9 3.9 %collective-permute-start.10 = (bf16[144,512]{1,0:T(8,128)(2,1)S(1)}, bf16[144,512]{1,0:T(8,128)(2,1)S(1)}, u32[]{:S(2)}, u32[]{:S(2)}) collective-permute-start(bf16[144,512]{1,0:T(8,128)(2,1)S(1)} %collective-permute-done.1.refs_0_.refs_10_), channel_id=1, source_target_pairs={{0,1},{1,0},{2,3},{3,2},{4,5},{5,4},{6,7},{7,6},{8,9},{9,8},{10,11... | collective-permute-start | bytes 442376 | tf_op jit(solution)/shard_map/ppermute | solution.py:36
  19.4 4.2 %collective-permute-start.12 = (bf16[144,512]{1,0:T(8,128)(2,1)S(1)}, bf16[144,512]{1,0:T(8,128)(2,1)S(1)}, u32[]{:S(2)}, u32[]{:S(2)}) collective-permute-start(bf16[144,512]{1,0:T(8,128)(2,1)S(1)} %collective-permute-done.11.refs_0_.refs_12_), channel_id=1, source_target_pairs={{0,1},{1,0},{2,3},{3,2},{4,5},{5,4},{6,7},{7,6},{8,9},{9,8},{10,11... | collective-permute-start | bytes 442376 | tf_op jit(solution)/shard_map/ppermute | solution.py:36
  20.1 4.4 %collective-permute-start.14 = (bf16[144,512]{1,0:T(8,128)(2,1)S(1)}, bf16[144,512]{1,0:T(8,128)(2,1)S(1)}, u32[]{:S(2)}, u32[]{:S(2)}) collective-permute-start(bf16[144,512]{1,0:T(8,128)(2,1)S(1)} %collective-permute-done.13.refs_0_.refs_14_), channel_id=1, source_target_pairs={{0,1},{1,0},{2,3},{3,2},{4,5},{5,4},{6,7},{7,6},{8,9},{9,8},{10,11... | collective-permute-start | bytes 442376 | tf_op jit(solution)/shard_map/ppermute | solution.py:36
  21.9 3.6 %collective-permute-start.3 = (bf16[144,512]{1,0:T(8,128)(2,1)S(1)}, bf16[144,512]{1,0:T(8,128)(2,1)S(1)}, u32[]{:S(2)}, u32[]{:S(2)}) collective-permute-start(bf16[144,512]{1,0:T(8,128)(2,1)S(1)} %collective-permute-done.2.refs_0_), channel_id=1, source_target_pairs={{0,1},{1,0},{2,3},{3,2},{4,5},{5,4},{6,7},{7,6},{8,9},{9,8},{10,11... | collective-permute-start | bytes 442376 | tf_op jit(solution)/shard_map/ppermute | solution.py:36

commit v3 on v2

--- a/solution.py
+++ b/solution.py
@@ -9,12 +9,11 @@
 
 AXES = ("blk", "pair", "sub")
 SMALL = (4, 2, 2)
-EVEN_MOVES = ((('pair', 1),), (('blk', 2),), (('blk', 1),))
-ODD_MOVES = ((('blk', 2),), (('blk', 1),), (('pair', 1),))
+EVEN_MOVES = (('pair', 1), ('blk', 2), ('blk', 1))
+ODD_MOVES = (('blk', 2), ('blk', 1), ('pair', 1))
 CHIP_MOVES = (("sub", 1),)
 SENDS = (('a', 'O', 0), ('b', 'O', 1), ('d', 'O', 2), ('c', 'a', 1), ('e', 'a', 2), ('f', 'b', 2), ('g', 'c', 2))
-STAGES = (('O',), ('a',), ('b',), ('d',), ('c',), ('e',), ('f',), ('g',))
-HELD = {}
+STAGES = (('O',), ('a', 'b'), ('d', 'e'), ('c', 'f'), ('g',))
 
 
 def swap_pairs(sizes, even_moves, odd_moves):
@@ -34,10 +33,6 @@
 
 def swapped(block, sizes, even_moves, odd_moves):
     return lax.ppermute(block, AXES, swap_pairs(sizes, even_moves, odd_moves))
-
-
-def joined(held, names):
-    return held[names] if names in held else jnp.concatenate([held[n] for n in names])
 
 
 def stage_call(news, olds, carry, g_rows, n_pairs, final):
@@ -95,12 +90,12 @@
         new_n = [jnp.concatenate(blocks_n[2 * i : 2 * i + 2], axis=1) for i in range(n_new)]
         lhs = rows * jnp.asarray(-2.0 / width, rows.dtype)
 
-        def spread(rhs, n_lane, count):
+        def spread(rhs, n_lane, begin, end):
             c = lax.dot_general(
-                lhs[0:count], rhs, (((1,), (1,)), ((), ())), preferred_element_type=jnp.float32
+                lhs[begin:end], rhs, (((1,), (1,)), ((), ())), preferred_element_type=jnp.float32
             )
-            lanes = c.shape[1]
-            n_row = jnp.concatenate([n_col[0:count]] * pl.cdiv(lanes, 128), axis=1)[:, 0:lanes]
+            count, lanes = c.shape
+            n_row = jnp.concatenate([n_col[begin:end]] * pl.cdiv(lanes, 128), axis=1)[:, 0:lanes]
             n_lane = jnp.broadcast_to(n_lane[None], (count // 8, 8, lanes)).reshape(count, lanes)
             return jnp.maximum((n_row + n_lane) + c, 1.0)
 
@@ -118,20 +113,28 @@
         loss = jnp.zeros((8, tile), jnp.float32)
         for i in range(n_old + n_new):
             if i < n_old:
+                begin = 0
                 rhs = jnp.concatenate([gens_of(old[2 * i]), gens_of(old[2 * i + 1])], axis=0)
-                s = spread(rhs, norms_in[i], gens_n + reals_n)
+                n_lane = norms_in[i]
             else:
-                j = i - n_old
-                s = spread(gens[j * tile : (j + 1) * tile], new_n[j], gens_n + reals_n)
+                begin = (i - n_old) * tile
+                rhs = gens[begin : begin + tile]
+                n_lane = new_n[i - n_old]
+            s = spread(rhs, n_lane, begin, gens_n + reals_n)
             w = lax.rsqrt(s)
             if i == 0:
                 pulled, w_sum = own_part(w)
             d = s * w
-            times = -2.0 if i < n_old else -1.0
-            loss += fold(d[0:gens_n]) * times + fold(d[gens_n:]) * (2.0 * ratio)
+            reals_at = gens_n - begin
+            loss += fold(d[reals_at:]) * (2.0 * ratio)
+            once = 0 if i < n_old else tile
+            if once:
+                loss += fold(d[0:once]) * -1.0
+            if once < reals_at:
+                loss += fold(d[once:reals_at]) * -2.0
         if not first:
             old_reals = jnp.concatenate([reals_of(b) for b in old], axis=0)
-            s = spread(old_reals, norms_in[n_pairs][:, 0 : old_reals.shape[0]], gens_n)
+            s = spread(old_reals, norms_in[n_pairs][:, 0 : old_reals.shape[0]], 0, gens_n)
             d = jnp.sum(fold(s * lax.rsqrt(s)), axis=1, keepdims=True) * (2.0 * ratio)
             lane = lax.broadcasted_iota(jnp.int32, (8, tile), 1)
             loss += jnp.where(lane == 0, d, 0.0)
@@ -188,31 +191,17 @@
     own = jnp.concatenate([generated, real], axis=0)
     g_rows, block_rows = generated.shape[0], own.shape[0]
     n_pairs = sizes[0] * sizes[1]
-    lane, chip = {"O": own}, {}
-    stages, seen, carry = [], [], ()
-
-    def held_back(name, value):
-        if name not in HELD:
-            return value
-        return lax.optimization_barrier((value, stages[HELD[name]][1]))[0]
-
-    def run_stages():
-        nonlocal seen, carry
-        while len(stages) < len(STAGES) and all(n in lane for n in STAGES[len(stages)]):
-            new = []
-            for n in STAGES[len(stages)]:
-                chip[n] = swapped(held_back("S" + n, lane[n]), sizes, CHIP_MOVES, CHIP_MOVES)
-                new += [lane[n], chip[n]]
-            final = len(stages) == len(STAGES) - 1
-            carry = stage_call(new, seen, carry, g_rows, n_pairs, final)
-            stages.append(carry)
-            seen = seen + new
-
-    run_stages()
-    for name, sources, move in SENDS:
-        block = held_back(name, joined(lane, sources))
-        lane[name] = swapped(block, sizes, EVEN_MOVES[move], ODD_MOVES[move])
-        run_stages()
+    lane = {"O": own}
+    for name, source, move in SENDS:
+        even, odd = EVEN_MOVES[move], ODD_MOVES[move]
+        lane[name] = swapped(lane[source], sizes, (even,), (odd,))
+    seen, carry = [], ()
+    for names in STAGES:
+        news = []
+        for name in names:
+            news += [lane[name], swapped(lane[name], sizes, CHIP_MOVES, CHIP_MOVES)]
+        carry = stage_call(news, seen, carry, g_rows, n_pairs, names == STAGES[-1])
+        seen = seen + news
     assert sum(b.shape[0] for b in seen) == 2 * n_pairs * block_rows
     return carry
 

time: 27.6 us -> 26.8 us (0.971)
  the two profiles are of different devices: /device:TPU:25 before, /device:TPU:0 now
where the time goes in v3:
time: 26.8 us; the launch traced here: 26.6 us
  starting transfers between devices  15.1 us (56%)
  Pallas kernels  6.52 us (24%)
  waiting for transfers between devices  3.42 us (13%)
  local copies, waits for them, and re-layouts  0.93 us (3%)
  between operations  0.69 us (3%)
    ppermute x15, starting transfers between devices, swapped(): return lax.ppermute(block, AXES, swap_pairs(sizes, even_moves, odd_moves))  15.1 us
    pallas_call x5, Pallas kernels, stage_call(): pl.pallas_call(kernel, out_shape=out_shape, in_specs=[vmem] * len(operand...  6.52 us
    ppermute x15, waiting for transfers between devices, swapped(): return lax.ppermute(block, AXES, swap_pairs(sizes, even_moves, odd_moves))  3.42 us
    unnamed x3, local copies, waits for them, and re-layouts  0.92 us
  transfers between devices with their start and end apart: 15, of which 4 were waited for; matrix products, arithmetic and copies ran while one was open for 0% of the time, Pallas kernels for 17%

profile of v3, /device:TPU:0, one launch (start us, length us, event | category | flops | bytes accessed | tf_op | source)
XLA Modules:
  0.0 26.6 jit_solution(17676003348493388880)
XLA Ops:
  0.6 0.0 copy-start
  0.6 0.9 %constant_dynamic-update-slice_fusion.1 = bf16[144,512]{1,0:T(8,128)(2,1)S(1)} fusion(bf16[128,512]{1,0:T(8,128)(2,1)} %param.2), kind=kLoop, calls=%fused_computation.1 | loop fusion | bytes 262144
  1.6 0.0 copy-done
  1.6 3.0 %collective-permute-start = (bf16[144,512]{1,0:T(8,128)(2,1)S(1)}, bf16[144,512]{1,0:T(8,128)(2,1)S(1)}, u32[]{:S(2)}, u32[]{:S(2)}) collective-permute-start(bf16[144,512]{1,0:T(8,128)(2,1)S(1)} %constant_dynamic-update-slice_fusion.refs_0_.refs_4_.refs_2_), channel_id=1, source_target_pairs={{0,2},{1,9},{2,0},{3,11},{4,6},{5,13},{6,4},{7,15},{8,10},{9,1},{1... | collective-permute-start | bytes 442376 | tf_op jit(solution)/shard_map/ppermute | solution.py:35
  4.6 0.7 %collective-permute-start.4 = (bf16[144,512]{1,0:T(8,128)(2,1)S(1)}, bf16[144,512]{1,0:T(8,128)(2,1)S(1)}, u32[]{:S(2)}, u32[]{:S(2)}) collective-permute-start(bf16[144,512]{1,0:T(8,128)(2,1)S(1)} %constant_dynamic-update-slice_fusion.refs_0_.refs_4_.refs_2_), channel_id=1, source_target_pairs={{0,1},{1,0},{2,3},{3,2},{4,5},{5,4},{6,7},{7,6},{8,9},{9,8},{10,11... | collective-permute-start | bytes 442376 | tf_op jit(solution)/shard_map/ppermute | solution.py:35
  5.2 1.9 %collective-permute-start.6 = (bf16[144,512]{1,0:T(8,128)(2,1)S(1)}, bf16[144,512]{1,0:T(8,128)(2,1)S(1)}, u32[]{:S(2)}, u32[]{:S(2)}) collective-permute-start(bf16[144,512]{1,0:T(8,128)(2,1)S(1)} %constant_dynamic-update-slice_fusion.refs_0_.refs_4_.refs_2_), channel_id=1, source_target_pairs={{0,8},{1,5},{2,10},{3,7},{4,12},{5,1},{6,14},{7,3},{8,0},{9,13},{1... | collective-permute-start | bytes 442376 | tf_op jit(solution)/shard_map/ppermute | solution.py:35
  7.2 1.6 %collective-permute-start.8 = (bf16[144,512]{1,0:T(8,128)(2,1)S(1)}, bf16[144,512]{1,0:T(8,128)(2,1)S(1)}, u32[]{:S(2)}, u32[]{:S(2)}) collective-permute-start(bf16[144,512]{1,0:T(8,128)(2,1)S(1)} %constant_dynamic-update-slice_fusion.refs_0_.refs_4_.refs_2_), channel_id=1, source_target_pairs={{0,4},{1,3},{2,6},{3,1},{4,0},{5,7},{6,2},{7,5},{8,12},{9,11},{10,... | collective-permute-start | bytes 442376 | tf_op jit(solution)/shard_map/ppermute | solution.py:35
  8.8 0.0 collective-permute-done.refs_0_.refs_6_.refs_4_
  8.8 2.1 %collective-permute-start.1 = (bf16[144,512]{1,0:T(8,128)(2,1)S(1)}, bf16[144,512]{1,0:T(8,128)(2,1)S(1)}, u32[]{:S(2)}, u32[]{:S(2)}) collective-permute-start(bf16[144,512]{1,0:T(8,128)(2,1)S(1)} %collective-permute-done.refs_0_.refs_6_.refs_4_), channel_id=1, source_target_pairs={{0,8},{1,5},{2,10},{3,7},{4,12},{5,1},{6,14},{7,3},{8,0},{9,13},{1... | collective-permute-start | bytes 442376 | tf_op jit(solution)/shard_map/ppermute | solution.py:35
  10.8 1.2 %collective-permute-start.5 = (bf16[144,512]{1,0:T(8,128)(2,1)S(1)}, bf16[144,512]{1,0:T(8,128)(2,1)S(1)}, u32[]{:S(2)}, u32[]{:S(2)}) collective-permute-start(bf16[144,512]{1,0:T(8,128)(2,1)S(1)} %collective-permute-done.refs_0_.refs_6_.refs_4_), channel_id=1, source_target_pairs={{0,1},{1,0},{2,3},{3,2},{4,5},{5,4},{6,7},{7,6},{8,9},{9,8},{10,11... | collective-permute-start | bytes 442376 | tf_op jit(solution)/shard_map/ppermute | solution.py:35
  12.0 0.0 collective-permute-done.4.refs_1_.refs_5_.refs_3_
  12.0 0.8 %collective-permute-start.10 = (bf16[144,512]{1,0:T(8,128)(2,1)S(1)}, bf16[144,512]{1,0:T(8,128)(2,1)S(1)}, u32[]{:S(2)}, u32[]{:S(2)}) collective-permute-start(bf16[144,512]{1,0:T(8,128)(2,1)S(1)} %collective-permute-done.refs_0_.refs_6_.refs_4_), channel_id=1, source_target_pairs={{0,4},{1,3},{2,6},{3,1},{4,0},{5,7},{6,2},{7,5},{8,12},{9,11},{10,... | collective-permute-start | bytes 442376 | tf_op jit(solution)/shard_map/ppermute | solution.py:35
  12.8 0.0 collective-permute-done.6.refs_2_.refs_8_.refs_6_
  12.8 1.5 %collective-permute-start.7 = (bf16[144,512]{1,0:T(8,128)(2,1)S(1)}, bf16[144,512]{1,0:T(8,128)(2,1)S(1)}, u32[]{:S(2)}, u32[]{:S(2)}) collective-permute-start(bf16[144,512]{1,0:T(8,128)(2,1)S(1)} %collective-permute-done.6.refs_2_.refs_8_.refs_6_), channel_id=1, source_target_pairs={{0,1},{1,0},{2,3},{3,2},{4,5},{5,4},{6,7},{7,6},{8,9},{9,8},{10,11... | collective-permute-start | bytes 442376 | tf_op jit(solution)/shard_map/ppermute | solution.py:35
  14.3 0.0 collective-permute-done.8.refs_0_.refs_10_.refs_8_
  14.3 1.2 %collective-permute-start.13 = (bf16[144,512]{1,0:T(8,128)(2,1)S(1)}, bf16[144,512]{1,0:T(8,128)(2,1)S(1)}, u32[]{:S(2)}, u32[]{:S(2)}) collective-permute-start(bf16[144,512]{1,0:T(8,128)(2,1)S(1)} %collective-permute-done.6.refs_2_.refs_8_.refs_6_), channel_id=1, source_target_pairs={{0,4},{1,3},{2,6},{3,1},{4,0},{5,7},{6,2},{7,5},{8,12},{9,11},{10,... | collective-permute-start | bytes 442376 | tf_op jit(solution)/shard_map/ppermute | solution.py:35
  15.5 1.1 %collective-permute-done.1.refs_0_.refs_12_ = bf16[144,512]{1,0:T(8,128)(2,1)S(1)} collective-permute-done((bf16[144,512]{1,0:T(8,128)(2,1)S(1)}, bf16[144,512]{1,0:T(8,128)(2,1)S(1)}, u32[]{:S(2)}, u32[]{:S(2)}) %collective-permute-start.1) | collective-permute-done | bytes 147488 | tf_op jit(solution)/shard_map/ppermute | solution.py:35
  16.5 0.2 collective-permute-start.2
  16.7 0.0 collective-permute-done.5.refs_1_.refs_7_.refs_5_
  16.7 0.5 %collective-permute-start.9 = (bf16[144,512]{1,0:T(8,128)(2,1)S(1)}, bf16[144,512]{1,0:T(8,128)(2,1)S(1)}, u32[]{:S(2)}, u32[]{:S(2)}) collective-permute-start(bf16[144,512]{1,0:T(8,128)(2,1)S(1)} %collective-permute-done.8.refs_0_.refs_10_.refs_8_), channel_id=1, source_target_pairs={{0,1},{1,0},{2,3},{3,2},{4,5},{5,4},{6,7},{7,6},{8,9},{9,8},{10,11... | collective-permute-start | bytes 442376 | tf_op jit(solution)/shard_map/ppermute | solution.py:35
  17.2 0.6 %collective-permute-done.10.refs_2_.refs_12_.refs_10_ = bf16[144,512]{1,0:T(8,128)(2,1)S(1)} collective-permute-done((bf16[144,512]{1,0:T(8,128)(2,1)S(1)}, bf16[144,512]{1,0:T(8,128)(2,1)S(1)}, u32[]{:S(2)}, u32[]{:S(2)}) %collective-permute-start.10) | collective-permute-done | bytes 147488 | tf_op jit(solution)/shard_map/ppermute | solution.py:35
  17.9 0.0 collective-permute-start.11
  17.9 0.0 collective-permute-done.7.refs_3_.refs_9_.refs_7_
  17.9 0.5 %collective-permute-start.12 = (bf16[144,512]{1,0:T(8,128)(2,1)S(1)}, bf16[144,512]{1,0:T(8,128)(2,1)S(1)}, u32[]{:S(2)}, u32[]{:S(2)}) collective-permute-start(bf16[144,512]{1,0:T(8,128)(2,1)S(1)} %collective-permute-done.1.refs_0_.refs_12_), channel_id=1, source_target_pairs={{0,1},{1,0},{2,3},{3,2},{4,5},{5,4},{6,7},{7,6},{8,9},{9,8},{10,11... | collective-permute-start | bytes 442376 | tf_op jit(solution)/shard_map/ppermute | solution.py:35
  18.4 1.1 %collective-permute-done.13.refs_2_.refs_14_ = bf16[144,512]{1,0:T(8,128)(2,1)S(1)} collective-permute-done((bf16[144,512]{1,0:T(8,128)(2,1)S(1)}, bf16[144,512]{1,0:T(8,128)(2,1)S(1)}, u32[]{:S(2)}, u32[]{:S(2)}) %collective-permute-start.13) | collective-permute-done | bytes 147488 | tf_op jit(solution)/shard_map/ppermute | solution.py:35
  19.4 0.0 collective-permute-start.14
  19.4 0.6 %shard_map.41 = (f32[128,512]{1,0:T(8,128)S(1)}, f32[16,256]{1,0:T(8,128)S(1)}, f32[9,8,256]{2,1,0:T(8,128)S(1)}) custom-call(bf16[144,512]{1,0:T(8,128)(2,1)S(1)} %constant_dynamic-update-slice_fusion.refs_0_.refs_4_.refs_2_, bf16[144,512]{1,0:T(8,128)(2,1)S(1)} %collective-permute-done.4.refs_1_.refs_5_.refs_3_), custom_call_target="tpu_custom_call" | custom-call | flops 75497472 | bytes 1024 | tf_op jit(solution)/shard_map/pallas_call | solution.py:178
  20.1 1.0 %shard_map.42 = (f32[128,512]{1,0:T(8,128)S(1)}, f32[16,256]{1,0:T(8,128)S(1)}, f32[9,8,256]{2,1,0:T(8,128)S(1)}) custom-call(bf16[144,512]{1,0:T(8,128)(2,1)S(1)} %collective-permute-done.refs_0_.refs_6_.refs_4_, bf16[144,512]{1,0:T(8,128)(2,1)S(1)} %collective-permute-done.5.refs_1_.refs_7_.refs_5_, ...), custom_call_target="tpu_custom_call" | custom-call | flops 471859200 | bytes 1024 | tf_op jit(solution)/shard_map/pallas_call | solution.py:178
  21.0 0.6 %collective-permute-done.2.refs_0_ = bf16[144,512]{1,0:T(8,128)(2,1)S(1)} collective-permute-done((bf16[144,512]{1,0:T(8,128)(2,1)S(1)}, bf16[144,512]{1,0:T(8,128)(2,1)S(1)}, u32[]{:S(2)}, u32[]{:S(2)}) %collective-permute-start.2) | collective-permute-done | bytes 147488 | tf_op jit(solution)/shard_map/ppermute | solution.py:35
  21.7 0.0 collective-permute-start.3
  21.7 0.0 collective-permute-done.9.refs_1_.refs_11_.refs_9_
  21.7 0.0 collective-permute-done.11.refs_3_.refs_13_.refs_11_
  21.7 1.3 %shard_map.43 = (f32[128,512]{1,0:T(8,128)S(1)}, f32[16,256]{1,0:T(8,128)S(1)}, f32[9,8,256]{2,1,0:T(8,128)S(1)}) custom-call(bf16[144,512]{1,0:T(8,128)(2,1)S(1)} %collective-permute-done.8.refs_0_.refs_10_.refs_8_, bf16[144,512]{1,0:T(8,128)(2,1)S(1)} %collective-permute-done.9.refs_1_.refs_11_.refs_9_, ...), custom_call_target="tpu_custom_call" | custom-call | flops 811597824 | bytes 1024 | tf_op jit(solution)/shard_map/pallas_call | solution.py:178
  23.0 0.0 collective-permute-done.12.refs_1_.refs_13_
  23.0 0.0 collective-permute-done.14.refs_3_.refs_15_
  23.0 1.7 %shard_map.44 = (f32[128,512]{1,0:T(8,128)S(1)}, f32[16,256]{1,0:T(8,128)S(1)}, f32[9,8,256]{2,1,0:T(8,128)S(1)}) custom-call(bf16[144,512]{1,0:T(8,128)(2,1)S(1)} %collective-permute-done.1.refs_0_.refs_12_, bf16[144,512]{1,0:T(8,128)(2,1)S(1)} %collective-permute-done.12.refs_1_.refs_13_, bf16[144,512]{1,0:T(8,128)(2,1)S(1)} %collective-permute-done.13.refs_2_.refs_14_, ...), custom_call_target="tpu_custom_call" | custom-call | flops 1151336448 | bytes 1024 | tf_op jit(solution)/shard_map/pallas_call | solution.py:178
  24.7 0.0 collective-permute-done.3.refs_1_
  24.7 1.9 %shard_map.45 = (f32[128,512]{1,0:T(8,128)}, f32[1]{0:T(128)}) custom-call(bf16[144,512]{1,0:T(8,128)(2,1)S(1)} %collective-permute-done.2.refs_0_, bf16[144,512]{1,0:T(8,128)(2,1)S(1)} %collective-permute-done.3.refs_1_, bf16[144,512]{1,0:T(8,128)(2,1)S(1)} %constant_dynamic-update-slice_fusion.refs_0_.refs_4_.refs_2_, ...), custom_call_target="tpu_custom_call" | custom-call | flops 670040064 | bytes 1024 | tf_op jit(solution)/shard_map/pallas_call | solution.py:178
  (1 shorter events, 0.0 us)
Async XLA Ops:
  0.6 0.9 %copy-start = (bf16[16,512]{1,0:T(8,128)(2,1)S(1)}, bf16[16,512]{1,0:T(8,128)(2,1)}, u32[]{:S(2)}) copy-start(bf16[16,512]{1,0:T(8,128)(2,1)} %param.3) | copy-start | bytes 49156
  1.6 7.2 %collective-permute-start = (bf16[144,512]{1,0:T(8,128)(2,1)S(1)}, bf16[144,512]{1,0:T(8,128)(2,1)S(1)}, u32[]{:S(2)}, u32[]{:S(2)}) collective-permute-start(bf16[144,512]{1,0:T(8,128)(2,1)S(1)} %constant_dynamic-update-slice_fusion.refs_0_.refs_4_.refs_2_), channel_id=1, source_target_pairs={{0,2},{1,9},{2,0},{3,11},{4,6},{5,13},{6,4},{7,15},{8,10},{9,1},{1... | collective-permute-start | bytes 442376 | tf_op jit(solution)/shard_map/ppermute | solution.py:35
  4.6 7.4 %collective-permute-start.4 = (bf16[144,512]{1,0:T(8,128)(2,1)S(1)}, bf16[144,512]{1,0:T(8,128)(2,1)S(1)}, u32[]{:S(2)}, u32[]{:S(2)}) collective-permute-start(bf16[144,512]{1,0:T(8,128)(2,1)S(1)} %constant_dynamic-update-slice_fusion.refs_0_.refs_4_.refs_2_), channel_id=1, source_target_pairs={{0,1},{1,0},{2,3},{3,2},{4,5},{5,4},{6,7},{7,6},{8,9},{9,8},{10,11... | collective-permute-start | bytes 442376 | tf_op jit(solution)/shard_map/ppermute | solution.py:35
  5.2 7.5 %collective-permute-start.6 = (bf16[144,512]{1,0:T(8,128)(2,1)S(1)}, bf16[144,512]{1,0:T(8,128)(2,1)S(1)}, u32[]{:S(2)}, u32[]{:S(2)}) collective-permute-start(bf16[144,512]{1,0:T(8,128)(2,1)S(1)} %constant_dynamic-update-slice_fusion.refs_0_.refs_4_.refs_2_), channel_id=1, source_target_pairs={{0,8},{1,5},{2,10},{3,7},{4,12},{5,1},{6,14},{7,3},{8,0},{9,13},{1... | collective-permute-start | bytes 442376 | tf_op jit(solution)/shard_map/ppermute | solution.py:35
  7.2 7.1 %collective-permute-start.8 = (bf16[144,512]{1,0:T(8,128)(2,1)S(1)}, bf16[144,512]{1,0:T(8,128)(2,1)S(1)}, u32[]{:S(2)}, u32[]{:S(2)}) collective-permute-start(bf16[144,512]{1,0:T(8,128)(2,1)S(1)} %constant_dynamic-update-slice_fusion.refs_0_.refs_4_.refs_2_), channel_id=1, source_target_pairs={{0,4},{1,3},{2,6},{3,1},{4,0},{5,7},{6,2},{7,5},{8,12},{9,11},{10,... | collective-permute-start | bytes 442376 | tf_op jit(solution)/shard_map/ppermute | solution.py:35
  8.8 7.8 %collective-permute-start.1 = (bf16[144,512]{1,0:T(8,128)(2,1)S(1)}, bf16[144,512]{1,0:T(8,128)(2,1)S(1)}, u32[]{:S(2)}, u32[]{:S(2)}) collective-permute-start(bf16[144,512]{1,0:T(8,128)(2,1)S(1)} %collective-permute-done.refs_0_.refs_6_.refs_4_), channel_id=1, source_target_pairs={{0,8},{1,5},{2,10},{3,7},{4,12},{5,1},{6,14},{7,3},{8,0},{9,13},{1... | collective-permute-start | bytes 442376 | tf_op jit(solution)/shard_map/ppermute | solution.py:35
  10.8 5.9 %collective-permute-start.5 = (bf16[144,512]{1,0:T(8,128)(2,1)S(1)}, bf16[144,512]{1,0:T(8,128)(2,1)S(1)}, u32[]{:S(2)}, u32[]{:S(2)}) collective-permute-start(bf16[144,512]{1,0:T(8,128)(2,1)S(1)} %collective-permute-done.refs_0_.refs_6_.refs_4_), channel_id=1, source_target_pairs={{0,1},{1,0},{2,3},{3,2},{4,5},{5,4},{6,7},{7,6},{8,9},{9,8},{10,11... | collective-permute-start | bytes 442376 | tf_op jit(solution)/shard_map/ppermute | solution.py:35
  12.0 5.9 %collective-permute-start.10 = (bf16[144,512]{1,0:T(8,128)(2,1)S(1)}, bf16[144,512]{1,0:T(8,128)(2,1)S(1)}, u32[]{:S(2)}, u32[]{:S(2)}) collective-permute-start(bf16[144,512]{1,0:T(8,128)(2,1)S(1)} %collective-permute-done.refs_0_.refs_6_.refs_4_), channel_id=1, source_target_pairs={{0,4},{1,3},{2,6},{3,1},{4,0},{5,7},{6,2},{7,5},{8,12},{9,11},{10,... | collective-permute-start | bytes 442376 | tf_op jit(solution)/shard_map/ppermute | solution.py:35
  12.8 5.1 %collective-permute-start.7 = (bf16[144,512]{1,0:T(8,128)(2,1)S(1)}, bf16[144,512]{1,0:T(8,128)(2,1)S(1)}, u32[]{:S(2)}, u32[]{:S(2)}) collective-permute-start(bf16[144,512]{1,0:T(8,128)(2,1)S(1)} %collective-permute-done.6.refs_2_.refs_8_.refs_6_), channel_id=1, source_target_pairs={{0,1},{1,0},{2,3},{3,2},{4,5},{5,4},{6,7},{7,6},{8,9},{9,8},{10,11... | collective-permute-start | bytes 442376 | tf_op jit(solution)/shard_map/ppermute | solution.py:35
  14.3 5.2 %collective-permute-start.13 = (bf16[144,512]{1,0:T(8,128)(2,1)S(1)}, bf16[144,512]{1,0:T(8,128)(2,1)S(1)}, u32[]{:S(2)}, u32[]{:S(2)}) collective-permute-start(bf16[144,512]{1,0:T(8,128)(2,1)S(1)} %collective-permute-done.6.refs_2_.refs_8_.refs_6_), channel_id=1, source_target_pairs={{0,4},{1,3},{2,6},{3,1},{4,0},{5,7},{6,2},{7,5},{8,12},{9,11},{10,... | collective-permute-start | bytes 442376 | tf_op jit(solution)/shard_map/ppermute | solution.py:35
  16.5 5.1 %collective-permute-start.2 = (bf16[144,512]{1,0:T(8,128)(2,1)S(1)}, bf16[144,512]{1,0:T(8,128)(2,1)S(1)}, u32[]{:S(2)}, u32[]{:S(2)}) collective-permute-start(bf16[144,512]{1,0:T(8,128)(2,1)S(1)} %collective-permute-done.1.refs_0_.refs_12_), channel_id=1, source_target_pairs={{0,4},{1,3},{2,6},{3,1},{4,0},{5,7},{6,2},{7,5},{8,12},{9,11},{10,... | collective-permute-start | bytes 442376 | tf_op jit(solution)/shard_map/ppermute | solution.py:35
  16.7 5.0 %collective-permute-start.9 = (bf16[144,512]{1,0:T(8,128)(2,1)S(1)}, bf16[144,512]{1,0:T(8,128)(2,1)S(1)}, u32[]{:S(2)}, u32[]{:S(2)}) collective-permute-start(bf16[144,512]{1,0:T(8,128)(2,1)S(1)} %collective-permute-done.8.refs_0_.refs_10_.refs_8_), channel_id=1, source_target_pairs={{0,1},{1,0},{2,3},{3,2},{4,5},{5,4},{6,7},{7,6},{8,9},{9,8},{10,11... | collective-permute-start | bytes 442376 | tf_op jit(solution)/shard_map/ppermute | solution.py:35
  17.9 3.8 %collective-permute-start.11 = (bf16[144,512]{1,0:T(8,128)(2,1)S(1)}, bf16[144,512]{1,0:T(8,128)(2,1)S(1)}, u32[]{:S(2)}, u32[]{:S(2)}) collective-permute-start(bf16[144,512]{1,0:T(8,128)(2,1)S(1)} %collective-permute-done.10.refs_2_.refs_12_.refs_10_), channel_id=1, source_target_pairs={{0,1},{1,0},{2,3},{3,2},{4,5},{5,4},{6,7},{7,6},{8,9},{9,8},{10,11... | collective-permute-start | bytes 442376 | tf_op jit(solution)/shard_map/ppermute | solution.py:35
  17.9 5.1 %collective-permute-start.12 = (bf16[144,512]{1,0:T(8,128)(2,1)S(1)}, bf16[144,512]{1,0:T(8,128)(2,1)S(1)}, u32[]{:S(2)}, u32[]{:S(2)}) collective-permute-start(bf16[144,512]{1,0:T(8,128)(2,1)S(1)} %collective-permute-done.1.refs_0_.refs_12_), channel_id=1, source_target_pairs={{0,1},{1,0},{2,3},{3,2},{4,5},{5,4},{6,7},{7,6},{8,9},{9,8},{10,11... | collective-permute-start | bytes 442376 | tf_op jit(solution)/shard_map/ppermute | solution.py:35
  19.4 3.6 %collective-permute-start.14 = (bf16[144,512]{1,0:T(8,128)(2,1)S(1)}, bf16[144,512]{1,0:T(8,128)(2,1)S(1)}, u32[]{:S(2)}, u32[]{:S(2)}) collective-permute-start(bf16[144,512]{1,0:T(8,128)(2,1)S(1)} %collective-permute-done.13.refs_2_.refs_14_), channel_id=1, source_target_pairs={{0,1},{1,0},{2,3},{3,2},{4,5},{5,4},{6,7},{7,6},{8,9},{9,8},{10,11... | collective-permute-start | bytes 442376 | tf_op jit(solution)/shard_map/ppermute | solution.py:35
  21.7 3.0 %collective-permute-start.3 = (bf16[144,512]{1,0:T(8,128)(2,1)S(1)}, bf16[144,512]{1,0:T(8,128)(2,1)S(1)}, u32[]{:S(2)}, u32[]{:S(2)}) collective-permute-start(bf16[144,512]{1,0:T(8,128)(2,1)S(1)} %collective-permute-done.2.refs_0_), channel_id=1, source_target_pairs={{0,1},{1,0},{2,3},{3,2},{4,5},{5,4},{6,7},{7,6},{8,9},{9,8},{10,11... | collective-permute-start | bytes 442376 | tf_op jit(solution)/shard_map/ppermute | solution.py:35

commit v4 on v3

--- a/solution.py
+++ b/solution.py
@@ -13,7 +13,8 @@
 ODD_MOVES = (('blk', 2), ('blk', 1), ('pair', 1))
 CHIP_MOVES = (("sub", 1),)
 SENDS = (('a', 'O', 0), ('b', 'O', 1), ('d', 'O', 2), ('c', 'a', 1), ('e', 'a', 2), ('f', 'b', 2), ('g', 'c', 2))
-STAGES = (('O',), ('a', 'b'), ('d', 'e'), ('c', 'f'), ('g',))
+STAGES = (('O',), ('a', 'b'), ('d', 'c'), ('e', 'f'), ('g',))
+STAGE_COSTS = (0.6, 1.0, 1.5, 1.0, 6.0)
 
 
 def swap_pairs(sizes, even_moves, odd_moves):
@@ -35,7 +36,7 @@
     return lax.ppermute(block, AXES, swap_pairs(sizes, even_moves, odd_moves))
 
 
-def stage_call(news, olds, carry, g_rows, n_pairs, final):
+def stage_call(news, olds, carry, g_rows, n_pairs, final, cost):
     step = olds[0].shape[0] if olds else news[0].shape[0]
     width = news[0].shape[1]
     r_rows = step - g_rows
@@ -181,7 +182,7 @@
         in_specs=[vmem] * len(operands),
         out_specs=out_specs,
         cost_estimate=pl.CostEstimate(
-            flops=int(2 * entries * width * 1), bytes_accessed=1024, transcendentals=entries
+            flops=int(2 * entries * width * cost), bytes_accessed=1024, transcendentals=entries
         ),
         compiler_params=pltpu.CompilerParams(vmem_limit_bytes=32 * 1024 * 1024),
     )(*operands)
@@ -196,11 +197,12 @@
         even, odd = EVEN_MOVES[move], ODD_MOVES[move]
         lane[name] = swapped(lane[source], sizes, (even,), (odd,))
     seen, carry = [], ()
-    for names in STAGES:
+    for names, cost in zip(STAGES, STAGE_COSTS, strict=True):
         news = []
         for name in names:
             news += [lane[name], swapped(lane[name], sizes, CHIP_MOVES, CHIP_MOVES)]
-        carry = stage_call(news, seen, carry, g_rows, n_pairs, names == STAGES[-1])
+        final = names == STAGES[-1]
+        carry = stage_call(news, seen, carry, g_rows, n_pairs, final, cost)
         seen = seen + news
     assert sum(b.shape[0] for b in seen) == 2 * n_pairs * block_rows
     return carry

time: 26.8 us -> 26.9 us (level)
  starting transfers between devices: 15.1 us -> 14.1 us
  waiting for transfers between devices: 3.42 us -> 4.26 us
    ppermute x15, starting transfers between devices: 15.1 us -> 14.1 us  [swapped(): return lax.ppermute(block, AXES, swap_pairs(sizes, even_moves, odd_moves))]
    ppermute x15, waiting for transfers between devices: 3.42 us -> 4.26 us  [swapped(): return lax.ppermute(block, AXES, swap_pairs(sizes, even_moves, odd_moves))]
where the time goes in v4:
time: 26.9 us; the launch traced here: 26.5 us
  starting transfers between devices  14.1 us (52%)
  Pallas kernels  6.53 us (24%)
  waiting for transfers between devices  4.26 us (16%)
  local copies, waits for them, and re-layouts  0.93 us (3%)
  between operations  0.69 us (3%)
    ppermute x15, starting transfers between devices, swapped(): return lax.ppermute(block, AXES, swap_pairs(sizes, even_moves, odd_moves))  14.1 us
    pallas_call x5, Pallas kernels, stage_call(): pl.pallas_call(kernel, out_shape=out_shape, in_specs=[vmem] * len(operand...  6.53 us
    ppermute x15, waiting for transfers between devices, swapped(): return lax.ppermute(block, AXES, swap_pairs(sizes, even_moves, odd_moves))  4.26 us
    unnamed x3, local copies, waits for them, and re-layouts  0.92 us
  transfers between devices with their start and end apart: 15, of which 4 were waited for; matrix products, arithmetic and copies ran while one was open for 0% of the time, Pallas kernels for 17%

profile of v4, /device:TPU:0, one launch (start us, length us, event | category | flops | bytes accessed | tf_op | source)
XLA Modules:
  0.0 26.5 jit_solution(7459923618586275797)
XLA Ops:
  0.6 0.0 copy-start
  0.6 0.9 %constant_dynamic-update-slice_fusion.1 = bf16[144,512]{1,0:T(8,128)(2,1)S(1)} fusion(bf16[128,512]{1,0:T(8,128)(2,1)} %param.2), kind=kLoop, calls=%fused_computation.1 | loop fusion | bytes 262144
  1.6 0.0 copy-done
  1.6 3.0 %collective-permute-start = (bf16[144,512]{1,0:T(8,128)(2,1)S(1)}, bf16[144,512]{1,0:T(8,128)(2,1)S(1)}, u32[]{:S(2)}, u32[]{:S(2)}) collective-permute-start(bf16[144,512]{1,0:T(8,128)(2,1)S(1)} %constant_dynamic-update-slice_fusion.refs_0_.refs_4_.refs_2_), channel_id=1, source_target_pairs={{0,2},{1,9},{2,0},{3,11},{4,6},{5,13},{6,4},{7,15},{8,10},{9,1},{1... | collective-permute-start | bytes 442376 | tf_op jit(solution)/shard_map/ppermute | solution.py:36
  4.6 2.6 %collective-permute-start.6 = (bf16[144,512]{1,0:T(8,128)(2,1)S(1)}, bf16[144,512]{1,0:T(8,128)(2,1)S(1)}, u32[]{:S(2)}, u32[]{:S(2)}) collective-permute-start(bf16[144,512]{1,0:T(8,128)(2,1)S(1)} %constant_dynamic-update-slice_fusion.refs_0_.refs_4_.refs_2_), channel_id=1, source_target_pairs={{0,8},{1,5},{2,10},{3,7},{4,12},{5,1},{6,14},{7,3},{8,0},{9,13},{1... | collective-permute-start | bytes 442376 | tf_op jit(solution)/shard_map/ppermute | solution.py:36
  7.2 0.0 collective-permute-start.4
  7.2 1.6 %collective-permute-start.8 = (bf16[144,512]{1,0:T(8,128)(2,1)S(1)}, bf16[144,512]{1,0:T(8,128)(2,1)S(1)}, u32[]{:S(2)}, u32[]{:S(2)}) collective-permute-start(bf16[144,512]{1,0:T(8,128)(2,1)S(1)} %constant_dynamic-update-slice_fusion.refs_0_.refs_4_.refs_2_), channel_id=1, source_target_pairs={{0,4},{1,3},{2,6},{3,1},{4,0},{5,7},{6,2},{7,5},{8,12},{9,11},{10,... | collective-permute-start | bytes 442376 | tf_op jit(solution)/shard_map/ppermute | solution.py:36
  8.8 0.0 collective-permute-done.refs_0_.refs_6_.refs_4_
  8.8 2.4 %collective-permute-start.1 = (bf16[144,512]{1,0:T(8,128)(2,1)S(1)}, bf16[144,512]{1,0:T(8,128)(2,1)S(1)}, u32[]{:S(2)}, u32[]{:S(2)}) collective-permute-start(bf16[144,512]{1,0:T(8,128)(2,1)S(1)} %collective-permute-done.refs_0_.refs_6_.refs_4_), channel_id=1, source_target_pairs={{0,8},{1,5},{2,10},{3,7},{4,12},{5,1},{6,14},{7,3},{8,0},{9,13},{1... | collective-permute-start | bytes 442376 | tf_op jit(solution)/shard_map/ppermute | solution.py:36
  11.2 0.0 collective-permute-start.5
  11.2 1.7 %collective-permute-done.6.refs_2_.refs_8_.refs_6_ = bf16[144,512]{1,0:T(8,128)(2,1)S(1)} collective-permute-done((bf16[144,512]{1,0:T(8,128)(2,1)S(1)}, bf16[144,512]{1,0:T(8,128)(2,1)S(1)}, u32[]{:S(2)}, u32[]{:S(2)}) %collective-permute-start.6) | collective-permute-done | bytes 147488 | tf_op jit(solution)/shard_map/ppermute | solution.py:36
  12.8 0.0 collective-permute-start.7
  12.8 0.0 collective-permute-done.4.refs_1_.refs_5_.refs_3_
  12.8 0.6 %collective-permute-start.11 = (bf16[144,512]{1,0:T(8,128)(2,1)S(1)}, bf16[144,512]{1,0:T(8,128)(2,1)S(1)}, u32[]{:S(2)}, u32[]{:S(2)}) collective-permute-start(bf16[144,512]{1,0:T(8,128)(2,1)S(1)} %collective-permute-done.refs_0_.refs_6_.refs_4_), channel_id=1, source_target_pairs={{0,4},{1,3},{2,6},{3,1},{4,0},{5,7},{6,2},{7,5},{8,12},{9,11},{10,... | collective-permute-start | bytes 442376 | tf_op jit(solution)/shard_map/ppermute | solution.py:36
  13.4 0.0 collective-permute-done.8.refs_0_.refs_10_.refs_8_
  13.4 1.8 %collective-permute-start.13 = (bf16[144,512]{1,0:T(8,128)(2,1)S(1)}, bf16[144,512]{1,0:T(8,128)(2,1)S(1)}, u32[]{:S(2)}, u32[]{:S(2)}) collective-permute-start(bf16[144,512]{1,0:T(8,128)(2,1)S(1)} %collective-permute-done.6.refs_2_.refs_8_.refs_6_), channel_id=1, source_target_pairs={{0,4},{1,3},{2,6},{3,1},{4,0},{5,7},{6,2},{7,5},{8,12},{9,11},{10,... | collective-permute-start | bytes 442376 | tf_op jit(solution)/shard_map/ppermute | solution.py:36
  15.2 1.2 %collective-permute-done.1.refs_2_.refs_12_.refs_10_ = bf16[144,512]{1,0:T(8,128)(2,1)S(1)} collective-permute-done((bf16[144,512]{1,0:T(8,128)(2,1)S(1)}, bf16[144,512]{1,0:T(8,128)(2,1)S(1)}, u32[]{:S(2)}, u32[]{:S(2)}) %collective-permute-start.1) | collective-permute-done | bytes 147488 | tf_op jit(solution)/shard_map/ppermute | solution.py:36
  16.4 0.6 %collective-permute-start.2 = (bf16[144,512]{1,0:T(8,128)(2,1)S(1)}, bf16[144,512]{1,0:T(8,128)(2,1)S(1)}, u32[]{:S(2)}, u32[]{:S(2)}) collective-permute-start(bf16[144,512]{1,0:T(8,128)(2,1)S(1)} %collective-permute-done.1.refs_2_.refs_12_.refs_10_), channel_id=1, source_target_pairs={{0,4},{1,3},{2,6},{3,1},{4,0},{5,7},{6,2},{7,5},{8,12},{9,11},{10,... | collective-permute-start | bytes 442376 | tf_op jit(solution)/shard_map/ppermute | solution.py:36
  16.9 0.0 collective-permute-done.5.refs_1_.refs_7_.refs_5_
  16.9 1.0 %collective-permute-start.9 = (bf16[144,512]{1,0:T(8,128)(2,1)S(1)}, bf16[144,512]{1,0:T(8,128)(2,1)S(1)}, u32[]{:S(2)}, u32[]{:S(2)}) collective-permute-start(bf16[144,512]{1,0:T(8,128)(2,1)S(1)} %collective-permute-done.8.refs_0_.refs_10_.refs_8_), channel_id=1, source_target_pairs={{0,1},{1,0},{2,3},{3,2},{4,5},{5,4},{6,7},{7,6},{8,9},{9,8},{10,11... | collective-permute-start | bytes 442376 | tf_op jit(solution)/shard_map/ppermute | solution.py:36
  18.0 0.0 collective-permute-done.7.refs_3_.refs_9_.refs_7_
  18.0 0.1 collective-permute-start.10
  18.0 0.6 %shard_map.41 = (f32[128,512]{1,0:T(8,128)S(1)}, f32[16,256]{1,0:T(8,128)S(1)}, f32[9,8,256]{2,1,0:T(8,128)S(1)}) custom-call(bf16[144,512]{1,0:T(8,128)(2,1)S(1)} %constant_dynamic-update-slice_fusion.refs_0_.refs_4_.refs_2_, bf16[144,512]{1,0:T(8,128)(2,1)S(1)} %collective-permute-done.4.refs_1_.refs_5_.refs_3_), custom_call_target="tpu_custom_call" | custom-call | flops 45298484 | bytes 1024 | tf_op jit(solution)/shard_map/pallas_call | solution.py:179
  18.6 0.0 collective-permute-done.11.refs_0_.refs_12_
  18.7 0.5 %collective-permute-start.12 = (bf16[144,512]{1,0:T(8,128)(2,1)S(1)}, bf16[144,512]{1,0:T(8,128)(2,1)S(1)}, u32[]{:S(2)}, u32[]{:S(2)}) collective-permute-start(bf16[144,512]{1,0:T(8,128)(2,1)S(1)} %collective-permute-done.11.refs_0_.refs_12_), channel_id=1, source_target_pairs={{0,1},{1,0},{2,3},{3,2},{4,5},{5,4},{6,7},{7,6},{8,9},{9,8},{10,11... | collective-permute-start | bytes 442376 | tf_op jit(solution)/shard_map/ppermute | solution.py:36
  19.2 0.4 %collective-permute-done.13.refs_2_.refs_14_ = bf16[144,512]{1,0:T(8,128)(2,1)S(1)} collective-permute-done((bf16[144,512]{1,0:T(8,128)(2,1)S(1)}, bf16[144,512]{1,0:T(8,128)(2,1)S(1)}, u32[]{:S(2)}, u32[]{:S(2)}) %collective-permute-start.13) | collective-permute-done | bytes 147488 | tf_op jit(solution)/shard_map/ppermute | solution.py:36
  19.6 0.0 collective-permute-start.14
  19.6 1.0 %shard_map.42 = (f32[128,512]{1,0:T(8,128)S(1)}, f32[16,256]{1,0:T(8,128)S(1)}, f32[9,8,256]{2,1,0:T(8,128)S(1)}) custom-call(bf16[144,512]{1,0:T(8,128)(2,1)S(1)} %collective-permute-done.refs_0_.refs_6_.refs_4_, bf16[144,512]{1,0:T(8,128)(2,1)S(1)} %collective-permute-done.5.refs_1_.refs_7_.refs_5_, ...), custom_call_target="tpu_custom_call" | custom-call | flops 471859200 | bytes 1024 | tf_op jit(solution)/shard_map/pallas_call | solution.py:179
  20.6 1.0 %collective-permute-done.2.refs_0_ = bf16[144,512]{1,0:T(8,128)(2,1)S(1)} collective-permute-done((bf16[144,512]{1,0:T(8,128)(2,1)S(1)}, bf16[144,512]{1,0:T(8,128)(2,1)S(1)}, u32[]{:S(2)}, u32[]{:S(2)}) %collective-permute-start.2) | collective-permute-done | bytes 147488 | tf_op jit(solution)/shard_map/ppermute | solution.py:36
  21.5 0.0 collective-permute-start.3
  21.5 0.0 collective-permute-done.9.refs_1_.refs_11_.refs_9_
  21.5 0.0 collective-permute-done.10.refs_3_.refs_13_.refs_11_
  21.5 1.3 %shard_map.43 = (f32[128,512]{1,0:T(8,128)S(1)}, f32[16,256]{1,0:T(8,128)S(1)}, f32[9,8,256]{2,1,0:T(8,128)S(1)}) custom-call(bf16[144,512]{1,0:T(8,128)(2,1)S(1)} %collective-permute-done.8.refs_0_.refs_10_.refs_8_, bf16[144,512]{1,0:T(8,128)(2,1)S(1)} %collective-permute-done.9.refs_1_.refs_11_.refs_9_, ...), custom_call_target="tpu_custom_call" | custom-call | flops 1217396736 | bytes 1024 | tf_op jit(solution)/shard_map/pallas_call | solution.py:179
  22.9 0.0 collective-permute-done.12.refs_1_.refs_13_
  22.9 0.0 collective-permute-done.14.refs_3_.refs_15_
  22.9 1.7 %shard_map.44 = (f32[128,512]{1,0:T(8,128)S(1)}, f32[16,256]{1,0:T(8,128)S(1)}, f32[9,8,256]{2,1,0:T(8,128)S(1)}) custom-call(bf16[144,512]{1,0:T(8,128)(2,1)S(1)} %collective-permute-done.11.refs_0_.refs_12_, bf16[144,512]{1,0:T(8,128)(2,1)S(1)} %collective-permute-done.12.refs_1_.refs_13_, bf16[144,512]{1,0:T(8,128)(2,1)S(1)} %collective-permute-done.13.refs_2_.refs_14_, ...), custom_call_target="tpu_custom_call" | custom-call | flops 1151336448 | bytes 1024 | tf_op jit(solution)/shard_map/pallas_call | solution.py:179
  24.6 0.0 collective-permute-done.3.refs_1_
  24.6 1.9 %shard_map.45 = (f32[128,512]{1,0:T(8,128)}, f32[1]{0:T(128)}) custom-call(bf16[144,512]{1,0:T(8,128)(2,1)S(1)} %collective-permute-done.2.refs_0_, bf16[144,512]{1,0:T(8,128)(2,1)S(1)} %collective-permute-done.3.refs_1_, bf16[144,512]{1,0:T(8,128)(2,1)S(1)} %constant_dynamic-update-slice_fusion.refs_0_.refs_4_.refs_2_, ...), custom_call_target="tpu_custom_call" | custom-call | flops 4020240384 | bytes 1024 | tf_op jit(solution)/shard_map/pallas_call | solution.py:179
  (1 shorter events, 0.0 us)
Async XLA Ops:
  0.6 0.9 %copy-start = (bf16[16,512]{1,0:T(8,128)(2,1)S(1)}, bf16[16,512]{1,0:T(8,128)(2,1)}, u32[]{:S(2)}) copy-start(bf16[16,512]{1,0:T(8,128)(2,1)} %param.3) | copy-start | bytes 49156
  1.6 7.2 %collective-permute-start = (bf16[144,512]{1,0:T(8,128)(2,1)S(1)}, bf16[144,512]{1,0:T(8,128)(2,1)S(1)}, u32[]{:S(2)}, u32[]{:S(2)}) collective-permute-start(bf16[144,512]{1,0:T(8,128)(2,1)S(1)} %constant_dynamic-update-slice_fusion.refs_0_.refs_4_.refs_2_), channel_id=1, source_target_pairs={{0,2},{1,9},{2,0},{3,11},{4,6},{5,13},{6,4},{7,15},{8,10},{9,1},{1... | collective-permute-start | bytes 442376 | tf_op jit(solution)/shard_map/ppermute | solution.py:36
  4.6 8.3 %collective-permute-start.6 = (bf16[144,512]{1,0:T(8,128)(2,1)S(1)}, bf16[144,512]{1,0:T(8,128)(2,1)S(1)}, u32[]{:S(2)}, u32[]{:S(2)}) collective-permute-start(bf16[144,512]{1,0:T(8,128)(2,1)S(1)} %constant_dynamic-update-slice_fusion.refs_0_.refs_4_.refs_2_), channel_id=1, source_target_pairs={{0,8},{1,5},{2,10},{3,7},{4,12},{5,1},{6,14},{7,3},{8,0},{9,13},{1... | collective-permute-start | bytes 442376 | tf_op jit(solution)/shard_map/ppermute | solution.py:36
  7.2 5.7 %collective-permute-start.4 = (bf16[144,512]{1,0:T(8,128)(2,1)S(1)}, bf16[144,512]{1,0:T(8,128)(2,1)S(1)}, u32[]{:S(2)}, u32[]{:S(2)}) collective-permute-start(bf16[144,512]{1,0:T(8,128)(2,1)S(1)} %constant_dynamic-update-slice_fusion.refs_0_.refs_4_.refs_2_), channel_id=1, source_target_pairs={{0,1},{1,0},{2,3},{3,2},{4,5},{5,4},{6,7},{7,6},{8,9},{9,8},{10,11... | collective-permute-start | bytes 442376 | tf_op jit(solution)/shard_map/ppermute | solution.py:36
  7.2 6.2 %collective-permute-start.8 = (bf16[144,512]{1,0:T(8,128)(2,1)S(1)}, bf16[144,512]{1,0:T(8,128)(2,1)S(1)}, u32[]{:S(2)}, u32[]{:S(2)}) collective-permute-start(bf16[144,512]{1,0:T(8,128)(2,1)S(1)} %constant_dynamic-update-slice_fusion.refs_0_.refs_4_.refs_2_), channel_id=1, source_target_pairs={{0,4},{1,3},{2,6},{3,1},{4,0},{5,7},{6,2},{7,5},{8,12},{9,11},{10,... | collective-permute-start | bytes 442376 | tf_op jit(solution)/shard_map/ppermute | solution.py:36
  8.8 7.6 %collective-permute-start.1 = (bf16[144,512]{1,0:T(8,128)(2,1)S(1)}, bf16[144,512]{1,0:T(8,128)(2,1)S(1)}, u32[]{:S(2)}, u32[]{:S(2)}) collective-permute-start(bf16[144,512]{1,0:T(8,128)(2,1)S(1)} %collective-permute-done.refs_0_.refs_6_.refs_4_), channel_id=1, source_target_pairs={{0,8},{1,5},{2,10},{3,7},{4,12},{5,1},{6,14},{7,3},{8,0},{9,13},{1... | collective-permute-start | bytes 442376 | tf_op jit(solution)/shard_map/ppermute | solution.py:36
  11.2 5.8 %collective-permute-start.5 = (bf16[144,512]{1,0:T(8,128)(2,1)S(1)}, bf16[144,512]{1,0:T(8,128)(2,1)S(1)}, u32[]{:S(2)}, u32[]{:S(2)}) collective-permute-start(bf16[144,512]{1,0:T(8,128)(2,1)S(1)} %collective-permute-done.refs_0_.refs_6_.refs_4_), channel_id=1, source_target_pairs={{0,1},{1,0},{2,3},{3,2},{4,5},{5,4},{6,7},{7,6},{8,9},{9,8},{10,11... | collective-permute-start | bytes 442376 | tf_op jit(solution)/shard_map/ppermute | solution.py:36
  12.8 5.1 %collective-permute-start.7 = (bf16[144,512]{1,0:T(8,128)(2,1)S(1)}, bf16[144,512]{1,0:T(8,128)(2,1)S(1)}, u32[]{:S(2)}, u32[]{:S(2)}) collective-permute-start(bf16[144,512]{1,0:T(8,128)(2,1)S(1)} %collective-permute-done.6.refs_2_.refs_8_.refs_6_), channel_id=1, source_target_pairs={{0,1},{1,0},{2,3},{3,2},{4,5},{5,4},{6,7},{7,6},{8,9},{9,8},{10,11... | collective-permute-start | bytes 442376 | tf_op jit(solution)/shard_map/ppermute | solution.py:36
  12.8 5.8 %collective-permute-start.11 = (bf16[144,512]{1,0:T(8,128)(2,1)S(1)}, bf16[144,512]{1,0:T(8,128)(2,1)S(1)}, u32[]{:S(2)}, u32[]{:S(2)}) collective-permute-start(bf16[144,512]{1,0:T(8,128)(2,1)S(1)} %collective-permute-done.refs_0_.refs_6_.refs_4_), channel_id=1, source_target_pairs={{0,4},{1,3},{2,6},{3,1},{4,0},{5,7},{6,2},{7,5},{8,12},{9,11},{10,... | collective-permute-start | bytes 442376 | tf_op jit(solution)/shard_map/ppermute | solution.py:36
  13.4 6.1 %collective-permute-start.13 = (bf16[144,512]{1,0:T(8,128)(2,1)S(1)}, bf16[144,512]{1,0:T(8,128)(2,1)S(1)}, u32[]{:S(2)}, u32[]{:S(2)}) collective-permute-start(bf16[144,512]{1,0:T(8,128)(2,1)S(1)} %collective-permute-done.6.refs_2_.refs_8_.refs_6_), channel_id=1, source_target_pairs={{0,4},{1,3},{2,6},{3,1},{4,0},{5,7},{6,2},{7,5},{8,12},{9,11},{10,... | collective-permute-start | bytes 442376 | tf_op jit(solution)/shard_map/ppermute | solution.py:36
  16.4 5.1 %collective-permute-start.2 = (bf16[144,512]{1,0:T(8,128)(2,1)S(1)}, bf16[144,512]{1,0:T(8,128)(2,1)S(1)}, u32[]{:S(2)}, u32[]{:S(2)}) collective-permute-start(bf16[144,512]{1,0:T(8,128)(2,1)S(1)} %collective-permute-done.1.refs_2_.refs_12_.refs_10_), channel_id=1, source_target_pairs={{0,4},{1,3},{2,6},{3,1},{4,0},{5,7},{6,2},{7,5},{8,12},{9,11},{10,... | collective-permute-start | bytes 442376 | tf_op jit(solution)/shard_map/ppermute | solution.py:36
  16.9 4.6 %collective-permute-start.9 = (bf16[144,512]{1,0:T(8,128)(2,1)S(1)}, bf16[144,512]{1,0:T(8,128)(2,1)S(1)}, u32[]{:S(2)}, u32[]{:S(2)}) collective-permute-start(bf16[144,512]{1,0:T(8,128)(2,1)S(1)} %collective-permute-done.8.refs_0_.refs_10_.refs_8_), channel_id=1, source_target_pairs={{0,1},{1,0},{2,3},{3,2},{4,5},{5,4},{6,7},{7,6},{8,9},{9,8},{10,11... | collective-permute-start | bytes 442376 | tf_op jit(solution)/shard_map/ppermute | solution.py:36
  18.0 3.6 %collective-permute-start.10 = (bf16[144,512]{1,0:T(8,128)(2,1)S(1)}, bf16[144,512]{1,0:T(8,128)(2,1)S(1)}, u32[]{:S(2)}, u32[]{:S(2)}) collective-permute-start(bf16[144,512]{1,0:T(8,128)(2,1)S(1)} %collective-permute-done.1.refs_2_.refs_12_.refs_10_), channel_id=1, source_target_pairs={{0,1},{1,0},{2,3},{3,2},{4,5},{5,4},{6,7},{7,6},{8,9},{9,8},{10,11... | collective-permute-start | bytes 442376 | tf_op jit(solution)/shard_map/ppermute | solution.py:36
  18.7 4.2 %collective-permute-start.12 = (bf16[144,512]{1,0:T(8,128)(2,1)S(1)}, bf16[144,512]{1,0:T(8,128)(2,1)S(1)}, u32[]{:S(2)}, u32[]{:S(2)}) collective-permute-start(bf16[144,512]{1,0:T(8,128)(2,1)S(1)} %collective-permute-done.11.refs_0_.refs_12_), channel_id=1, source_target_pairs={{0,1},{1,0},{2,3},{3,2},{4,5},{5,4},{6,7},{7,6},{8,9},{9,8},{10,11... | collective-permute-start | bytes 442376 | tf_op jit(solution)/shard_map/ppermute | solution.py:36
  19.6 3.3 %collective-permute-start.14 = (bf16[144,512]{1,0:T(8,128)(2,1)S(1)}, bf16[144,512]{1,0:T(8,128)(2,1)S(1)}, u32[]{:S(2)}, u32[]{:S(2)}) collective-permute-start(bf16[144,512]{1,0:T(8,128)(2,1)S(1)} %collective-permute-done.13.refs_2_.refs_14_), channel_id=1, source_target_pairs={{0,1},{1,0},{2,3},{3,2},{4,5},{5,4},{6,7},{7,6},{8,9},{9,8},{10,11... | collective-permute-start | bytes 442376 | tf_op jit(solution)/shard_map/ppermute | solution.py:36
  21.5 3.0 %collective-permute-start.3 = (bf16[144,512]{1,0:T(8,128)(2,1)S(1)}, bf16[144,512]{1,0:T(8,128)(2,1)S(1)}, u32[]{:S(2)}, u32[]{:S(2)}) collective-permute-start(bf16[144,512]{1,0:T(8,128)(2,1)S(1)} %collective-permute-done.2.refs_0_), channel_id=1, source_target_pairs={{0,1},{1,0},{2,3},{3,2},{4,5},{5,4},{6,7},{7,6},{8,9},{9,8},{10,11... | collective-permute-start | bytes 442376 | tf_op jit(solution)/shard_map/ppermute | solution.py:36
